TPU v7x, 256 devices: a whole 4x4x8 slice. The times are simulated.
256 devices in a mesh: rep: 32 (over x_lo, z, core), tp: 8 (over x_hi, y).
Axes of the slice: x: 4 (x_hi: 2, x_lo: 2; x = x_hi * 2 + x_lo), y: 4, z: 8, core: 2. Of those that a mesh axis runs over, the one named last changes fastest.
Arguments:
- prefill_x: bfloat16 [8192, 8192], P('rep', 'tp'), as said below
- decode_x: bfloat16 [48, 8192], P(None, 'tp'), as said below
- query_weight: bfloat16 [8192, 8192], P('rep', 'tp'), may hold values from -0.125 to 0.125
- keyvalue_weight: bfloat16 [8192, 2048], P('rep', 'tp'), may hold values from -0.0625 to 0.0625
- key_cache: bfloat16 [48, 4096, 1024], P(None, 'rep', 'tp'), as said below
- value_cache: bfloat16 [48, 4096, 1024], P(None, 'rep', 'tp'), may hold values from -6 to 6
- cache_lengths: int32 [48], replicated, may hold values from 1 to 4096, as said below
- chain_order: int32 [32], replicated, may hold values from 0 to 31, each once
Outputs:
- prefill_attn: bfloat16 [8192, 8192], P('rep', 'tp')
- decode_attn: bfloat16 [48, 8192], P(None, 'tp')
Inputs may be any that keep to these rules, and one draw needn't show every extreme that they name: `cache_lengths`: every decode row holds 1 to 4096 cached positions, and some row holds exactly 4096. `chain_order`: each stored block appears once. `prefill_x`: of order one. `decode_x`: of order one. `key_cache`: of order one.
All inputs are finite; a program needn't handle non-finite values.
Results may differ from a plain program's by a relative error of at most 0.012.
The roundings to bfloat16 on the way count: a program that leaves them out, or rounds other values in their place, can miss the bound.
Values may be sent and summed in bfloat16 or wider, within the bound.
No kernel may reach another device: no remote copies, remote signals or barrier semaphores. Data moves between devices by JAX's collectives and lax.ppermute only.
A program may use at most 128 MiB of HBM per device.

v0:
```python
import math

import jax
import jax.numpy as jnp
from jax import lax
from jax.sharding import PartitionSpec as P

HD = 128
SEQ_LEN = 128


negative_big = -1e30


def combined_all(shard, axis, combine):
    everything = jax.tree.map(lambda part: lax.all_gather(part, axis), shard)
    leading = jax.tree.map(lambda part: part[0], everything)

    def turn(k, so_far):
        return combine(so_far, jax.tree.map(lambda part: part[k], everything))

    return lax.fori_loop(1, lax.axis_size(axis), turn, leading)


def prefill_attention(queries, keyvalues):
    token_rows = queries.shape[0]
    seq_count = token_rows // SEQ_LEN
    kv_heads = keyvalues.shape[1] // (2 * HD)
    grouped = queries.shape[1] // (HD * kv_heads)
    query_blocks = queries.reshape(seq_count, SEQ_LEN, kv_heads, grouped, HD)
    pairs = keyvalues.reshape(seq_count, SEQ_LEN, kv_heads, 2, HD)
    scores = jnp.einsum(
        "nqhgd,nkhd->nhgqk", query_blocks, pairs[:, :, :, 0], preferred_element_type=jnp.float32
    ) * (1.0 / math.sqrt(HD))
    causal = jnp.arange(SEQ_LEN)[:, None] >= jnp.arange(SEQ_LEN)[None, :]
    scores = jnp.where(causal, scores, negative_big)
    highest = jnp.max(scores, axis=-1, keepdims=True)
    expos = jnp.where(causal, jnp.exp(scores - highest), 0.0)
    sums = jnp.sum(expos, axis=-1)
    weighted = (
        jnp.einsum(
            "nhgqk,nkhd->nhgqd",
            expos.astype(jnp.bfloat16),
            pairs[:, :, :, 1],
            preferred_element_type=jnp.float32,
        )
        / sums[..., None]
    )
    return (
        weighted.astype(jnp.bfloat16)
        .transpose(0, 3, 1, 2, 4)
        .reshape(token_rows, kv_heads * grouped * HD)
    )


def combine_softmax(first, second):
    first_out, first_max, first_sum = first
    second_out, second_max, second_sum = second
    highest = jnp.maximum(first_max, second_max)
    first_keep = jnp.exp(first_max - highest)
    second_keep = jnp.exp(second_max - highest)
    merged_out = first_out * first_keep[..., None] + second_out * second_keep[..., None]
    return (merged_out, highest, first_sum * first_keep + second_sum * second_keep)


def decode_attention(queries, keyvalues, key_cache, value_cache, lengths):
    batch_rows = queries.shape[0]
    kv_heads = keyvalues.shape[1] // (2 * HD)
    grouped = queries.shape[1] // (HD * kv_heads)
    scaling = 1.0 / math.sqrt(HD)
    query_blocks = queries.reshape(batch_rows, kv_heads, grouped, HD)
    pairs = keyvalues.reshape(batch_rows, kv_heads, 2, HD)
    positions_here = key_cache.shape[1]
    cached_keys = key_cache.reshape(batch_rows, positions_here, kv_heads, HD)
    cached_values = value_cache.reshape(batch_rows, positions_here, kv_heads, HD)
    scores = (
        jnp.einsum("bhgd,bphd->bhgp", query_blocks, cached_keys, preferred_element_type=jnp.float32)
        * scaling
    )
    position = lax.axis_index("rep") * positions_here + jnp.arange(positions_here, dtype=jnp.int32)
    allowed = (position[None, :] < lengths[:, None])[:, None, None, :]
    local_max = jnp.max(jnp.where(allowed, scores, negative_big), axis=-1)
    expos = jnp.where(allowed, jnp.exp(scores - local_max[..., None]), 0.0)
    local_sum = jnp.sum(expos, axis=-1)
    local_out = jnp.einsum(
        "bhgp,bphd->bhgd",
        expos.astype(jnp.bfloat16),
        cached_values,
        preferred_element_type=jnp.float32,
    )
    merged_out, merged_max, merged_sum = combined_all(
        (local_out, local_max, local_sum), "rep", combine_softmax
    )
    own = (
        jnp.einsum(
            "bhgd,bhd->bhg", query_blocks, pairs[:, :, 0], preferred_element_type=jnp.float32
        )
        * scaling
    )
    highest = jnp.maximum(merged_max, own)
    keeping = jnp.exp(merged_max - highest)
    own_exp = jnp.exp(own - highest)
    numer = (
        merged_out * keeping[..., None]
        + own_exp.astype(jnp.bfloat16).astype(jnp.float32)[..., None]
        * pairs[:, :, 1].astype(jnp.float32)[:, :, None, :]
    )
    denom = merged_sum * keeping + own_exp
    return (
        (numer / denom[..., None]).astype(jnp.bfloat16).reshape(batch_rows, kv_heads * grouped * HD)
    )


def per_device(
    prefill_x,
    decode_x,
    query_weight,
    keyvalue_weight,
    key_cache,
    value_cache,
    cache_lengths,
    chain_order,
):
    groups = lax.axis_size("rep")
    block_rows = query_weight.shape[0]
    full_pre, full_dec = (
        lax.all_gather(prefill_x, "tp", axis=1, tiled=True),
        lax.all_gather(decode_x, "tp", axis=1, tiled=True),
    )
    tokens_here = full_pre.shape[0]
    rows_all = jnp.concatenate([full_pre, full_dec], axis=0)
    row_count = rows_all.shape[0]
    full_width = rows_all.shape[1]
    inverse = jnp.argsort(chain_order)
    stored = rows_all.reshape(row_count, groups, block_rows)[:, inverse, :].reshape(
        row_count, full_width
    )

    def add_rows(weight_piece):
        return jnp.dot(stored, weight_piece, preferred_element_type=jnp.float32)

    query_sum = add_rows(lax.all_gather(query_weight, "rep", axis=0, tiled=True))
    pair_sum = add_rows(lax.all_gather(keyvalue_weight, "rep", axis=0, tiled=True))
    queries = query_sum.astype(jnp.bfloat16)
    keyvalues = pair_sum.astype(jnp.bfloat16)
    attn_pre = prefill_attention(queries[:tokens_here], keyvalues[:tokens_here])
    attn_dec = decode_attention(
        queries[tokens_here:], keyvalues[tokens_here:], key_cache, value_cache, cache_lengths
    )
    return (attn_pre, attn_dec)


def solution(mesh):
    in_specs = (
        P("rep", "tp"),
        P(None, "tp"),
        P("rep", "tp"),
        P("rep", "tp"),
        P(None, "rep", "tp"),
        P(None, "rep", "tp"),
        P(),
        P(),
    )
    out_specs = (P("rep", "tp"), P(None, "tp"))
    return jax.shard_map(
        per_device, mesh=mesh, in_specs=in_specs, out_specs=out_specs, check_vma=False
    )
```

profile of v0, /device:TPU:1, one launch (start us, length us, event | category | flops | bytes accessed | tf_op | source)
XLA Modules:
  0.0 387.4 jit_solution(2795833661886019239)
XLA Ops:
  9.5 2.3 sort.17
  12.5 32.4 %all_gather.31 = bf16[48,8192]{1,0:T(8,128)(2,1)S(1)} all-gather(bf16[48,1024]{1,0:T(8,128)(2,1)} %param.11), channel_id=1, replica_groups=mesh['rep'=32,'tp'=8] {'tp'}, dimensions={1}, use_global_device_ids=true | all-gather | bytes 884736 | tf_op jit(solution)/shard_map/all_gather | solution.py:128
  44.9 48.5 %all-gather.10.cloned.1.call-done = bf16[256,8192]{1,0:T(8,128)(2,1)} async-done(((bf16[256,1024]{1,0:T(8,128)(2,1)}), bf16[256,8192]{1,0:T(8,128)(2,1)}) %all-gather.10.cloned.1.call-update) | async-done | bytes 4194320 | tf_op jit(solution)/shard_map/all_gather | solution.py:127
  93.3 2.5 pad_maximum_fusion
  95.8 2.5 copy.97
  98.4 5.5 %gather_fusion = bf16[32,304,256]{2,1,0:T(8,128)(2,1)} fusion(bf16[304,32,256]{2,0,1:T(8,128)(2,1)} %bitcast.132, s32[1024]{0:T(1024)S(1)} %pad_clamp_fusion), kind=kCustom, calls=%fused_computation | custom fusion | bytes 9961600 | tf_op jit(solution)/shard_map/gather | solution.py:135
  103.9 5.6 %copy.76 = bf16[32,38,8,256]{3,2,0,1:T(8,128)(2,1)} copy(bf16[32,38,8,256]{3,2,1,0:T(8,128)(2,1)} %bitcast.133) | data formatting | bytes 9961472 | tf_op jit(solution)/shard_map/reshape | solution.py:135
  109.5 84.2 %all-gather.14.cloned.1.call-done = bf16[8192,1024]{1,0:T(8,128)(2,1)} async-done(((bf16[256,1024]{1,0:T(8,128)(2,1)}), bf16[8192,1024]{1,0:T(8,128)(2,1)}) %all-gather.14.cloned.1.call-update) | async-done | bytes 16777232 | tf_op jit(solution)/shard_map/all_gather | solution.py:142
  193.7 12.1 %convolution_convert_fusion = bf16[304,1024]{1,0:T(8,128)(2,1)S(1)} fusion(bf16[304,8192]{1,0:T(8,128)(2,1)} %bitcast.134, bf16[8192,1024]{1,0:T(8,128)(2,1)} %all-gather.14.cloned.1.call-done), kind=kOutput, calls=%fused_computation.18 | convolution fusion | flops 5100584960 | bytes 22380544 | tf_op jit(solution)/shard_map/dot_general | solution.py:140
  205.9 1.0 select_reduce_fusion
  206.9 1.3 fusion.19
  208.2 54.6 %all-gather.12.cloned.1.call-done = bf16[8192,256]{1,0:T(8,128)(2,1)} async-done(((bf16[256,256]{1,0:T(8,128)(2,1)}), bf16[8192,256]{1,0:T(8,128)(2,1)}) %all-gather.12.cloned.1.call-update) | async-done | bytes 4194320 | tf_op jit(solution)/shard_map/all_gather | solution.py:143
  262.8 5.1 %convolution_convert_fusion.1 = bf16[304,256]{1,0:T(8,128)(2,1)S(1)} fusion(bf16[304,8192]{1,0:T(8,128)(2,1)} %bitcast.135, bf16[8192,256]{1,0:T(8,128)(2,1)} %all-gather.12.cloned.1.call-done), kind=kOutput, calls=%fused_computation.22 | convolution fusion | flops 1275146240 | bytes 9330688 | tf_op jit(solution)/shard_map/dot_general | solution.py:140
  268.6 32.8 %all-gather.4 = f32[32,48,8]{1,2,0:T(8,128)S(1)} all-gather(f32[1,48,8]{1,2,0:T(8,128)S(1)} %copy.57), channel_id=4, replica_groups=mesh['rep'=32,'tp'=8] {'rep'}, dimensions={0}, use_global_device_ids=true | all-gather | bytes 50688 | tf_op jit(solution)/shard_map/all_gather | solution.py:16
  301.6 31.2 %all-gather.3 = f32[32,48,8]{1,2,0:T(8,128)S(1)} all-gather(f32[1,48,8]{1,2,0:T(8,128)S(1)} %copy.56), channel_id=3, replica_groups=mesh['rep'=32,'tp'=8] {'rep'}, dimensions={0}, use_global_device_ids=true | all-gather | bytes 50688 | tf_op jit(solution)/shard_map/all_gather | solution.py:16
  335.5 0.9 slice_bitcast_fusion.1
  336.4 43.5 %while.19 = (s32[]{:T(128)}, f32[48,1,8,128]{3,2,1,0:T(8,128)S(1)}, f32[48,1,8]{2,0,1:T(8,128)S(1)}, f32[48,1,8]{2,0,1:T(8,128)S(1)}, f32[32,48,1,8]{1,3,0,2:T(8...) while((s32[]{:T(128)}, f32[48,1,8,128]{3,2,1,0:T(8,128)S(1)}, ...), condition=%wide.region_6.7_spmd, body=%wide.region_5.6_spmd.sunk | while | flops 150533 | bytes 625303 | solution.py:22
  336.7 1.1 fusion.46
  338.1 1.1 fusion.46
  339.5 1.1 fusion.46
  340.9 1.1 fusion.46
  342.3 1.1 fusion.46
  343.7 1.1 fusion.46
  345.1 1.1 fusion.46
  346.5 1.1 fusion.46
  347.9 1.1 fusion.46
  349.3 1.1 fusion.46
  350.7 1.1 fusion.46
  352.1 1.1 fusion.46
  353.5 1.1 fusion.46
  354.9 1.1 fusion.46
  356.3 1.1 fusion.46
  357.8 1.1 fusion.46
  359.2 1.1 fusion.46
  360.6 1.1 fusion.46
  362.0 1.1 fusion.46
  363.4 1.1 fusion.46
  364.8 1.1 fusion.46
  366.2 1.1 fusion.46
  367.6 1.1 fusion.46
  369.0 1.1 fusion.46
  370.4 1.1 fusion.46
  371.8 1.1 fusion.46
  373.2 1.1 fusion.46
  374.6 1.1 fusion.46
  376.0 1.1 fusion.46
  377.4 1.1 fusion.46
  378.8 1.1 fusion.46
  (232 shorter events, 13.9 us)
Async XLA Ops:
  7.2 198.7 %copy-start = (bf16[48,128,128]{2,1,0:T(8,128)(2,1)S(1)}, bf16[48,128,128]{2,1,0:T(8,128)(2,1)}, u32[]{:S(2)}) copy-start(bf16[48,128,128]{2,1,0:T(8,128)(2,1)} %param.14) | copy-start | bytes 4718596
  7.2 86.1 %all-gather.10.cloned.1.call-start = ((), (), s32[]{:S(2)}) async-start(), calls=%async_computation | async-start | bytes 4718592 | tf_op jit(solution)/shard_map/all_gather | solution.py:127
  7.9 185.8 %all-gather.14.cloned.1.call-start = ((), (), s32[]{:S(2)}) async-start(), calls=%async_computation.2 | async-start | bytes 17301504 | tf_op jit(solution)/shard_map/all_gather | solution.py:142
  8.7 254.1 %all-gather.12.cloned.1.call-start = ((), (), s32[]{:S(2)}) async-start(), calls=%async_computation.1 | async-start | bytes 4325376 | tf_op jit(solution)/shard_map/all_gather | solution.py:143
  9.4 326.1 %all-gather.16.cloned.1.call-start = ((), (), s32[]{:S(2)}) async-start(), calls=%async_computation.3 | async-start | bytes 6488064 | tf_op jit(solution)/shard_map/all_gather | solution.py:16
  193.7 13.2 %copy-start.1 = (bf16[48,128,128]{2,1,0:T(8,128)(2,1)S(1)}, bf16[48,128,128]{2,1,0:T(8,128)(2,1)}, u32[]{:S(2)}) copy-start(bf16[48,128,128]{2,1,0:T(8,128)(2,1)} %param.15) | copy-start | bytes 4718596
Sparse Core Ops, SparseCore 0:
  10.6 82.6 all-gather.9
  95.2 98.4 all-gather.13
  195.6 67.1 all-gather.11
  264.5 69.9 all-gather.15
where the time goes:
time: 388 us; the launch traced here: 387 us
  waiting for transfers between devices  189 us (49%)
  blocking collectives  96.4 us (25%)
  other arithmetic  42.8 us (11%)
  local copies, waits for them, and re-layouts  22.6 us (6%)
  matrix products  20.6 us (5%)
  between operations  14 us (4%)
    all_gather x1, waiting for transfers between devices, per_device(): lax.all_gather(query_weight, 'rep', axis=0, tiled=True)  84.2 us
    all_gather x2, blocking collectives, combined_all(): everything = jax.tree.map(lambda part: lax.all_gather(part, axis), shard)  64 us
    all_gather x1, waiting for transfers between devices, per_device(): lax.all_gather(keyvalue_weight, 'rep', axis=0, tiled=True)  54.6 us
    all_gather x1, waiting for transfers between devices, per_device(): lax.all_gather(prefill_x, 'tp', axis=1, tiled=True)  48.5 us
    add x31, other arithmetic, combine_softmax(): first_out * first_keep[..., None] + second_out * second_keep[..., None]  35.4 us
    all_gather x1, blocking collectives, per_device(): lax.all_gather(decode_x, 'tp', axis=1, tiled=True)  32.4 us
    dot_general x2, matrix products, add_rows(): return jnp.dot(stored, weight_piece, preferred_element_type=jnp.float32)  17.3 us
    reshape x2, local copies, waits for them, and re-layouts, per_device(): rows_all.reshape(row_count, groups, block_rows)[:, inverse, :]  8.12 us
  transfers between devices with their start and end apart: 4, of which 3 were waited for; matrix products, arithmetic and copies ran while one was open for 11% of the time, Pallas kernels for 0%

commit v1 on v0

v1 whole, which is shorter than its diff:
```python
import functools
import math

import jax
import jax.numpy as jnp
import numpy as np
from jax import lax
from jax.experimental import pallas as pl
from jax.experimental.pallas import tpu as pltpu
from jax.sharding import Mesh
from jax.sharding import PartitionSpec as P

HD = 128
SEQ_LEN = 128
HEADS = 8
BATCH = 48
ROWS = 256
WIDTH = 1024
HALF = 640
SCALE = 1.0 / math.sqrt(HD)
REP = ("xl", "z", "c")
X = ("xl", "xh")
negative_big = -1e30
PER_STEP = 4


def flat_x(x):
    return (x % 2) * 2 + x // 2


def ring(value, axes, size, shift):
    pairs = [(i, (i + shift) % size) for i in range(size)]
    if axes == X:
        pairs = [(flat_x(i), flat_x(j)) for i, j in pairs]
    return lax.ppermute(value, axes, pairs)


def around(value, axes, cut):
    before = ring(value, axes, 4, 1)
    after = ring(value, axes, 4, -1)
    far_top = ring(before[:cut], axes, 4, 1)
    far_low = ring(after[cut:], axes, 4, -1)
    return jnp.concatenate([value, before, after, far_top, far_low], axis=0)


def slot_of(place, here):
    gap = (place - here) % 4
    return jnp.where(gap == 0, 0, jnp.where(gap == 3, 1, jnp.where(gap == 1, 2, 3)))


def project_kernel(col_ref, sy_ref, sp_ref, so_ref, sd_ref, xa_ref, xb_ref, w1_ref, w2_ref, out_ref, acc):
    step = pl.program_id(0)
    steps = pl.num_programs(0)

    @pl.when(step == 0)
    def _():
        acc[...] = jnp.zeros_like(acc)

    def add(w_ref):
        total = None
        for k in range(PER_STEP):
            j = step * PER_STEP + k
            cols = pl.ds(pl.multiple_of(col_ref[j] * 256, 256), 256)
            sy = sy_ref[j]
            sp = pl.ds(pl.multiple_of(sp_ref[j] * 128, 128), 128)
            so = pl.ds(pl.multiple_of(so_ref[j] * 128, 128), 128)
            sd = pl.ds(pl.multiple_of(512 + sd_ref[j] * 48, 16), 48)
            sy_rows = pl.ds(pl.multiple_of(sy * 128, 128), 128)
            lhs = jnp.concatenate(
                [
                    xa_ref[sy, sp, cols],
                    xb_ref[sp_ref[j], sy_rows, cols],
                    xa_ref[sy, sd, cols],
                    xa_ref[sy, so, cols],
                    xb_ref[so_ref[j], sy_rows, cols],
                ],
                axis=0,
            )
            part = jnp.dot(lhs, w_ref[k], preferred_element_type=jnp.float32)
            total = part if total is None else total + part
        acc[...] += total

    @pl.when(step < steps // 2)
    def _():
        add(w1_ref)

    @pl.when(step >= steps // 2)
    def _():
        add(w2_ref)

    @pl.when(step == steps - 1)
    def _():
        out_ref[...] = acc[...].astype(out_ref.dtype)


def project(tables, xa, xb, w1, w2):
    steps = 32 // PER_STEP
    half = steps // 2
    rows = 2 * ROWS + BATCH
    whole = lambda shape: pl.BlockSpec(shape, lambda s, *_: (0,) * len(shape), pipeline_mode=pl.Buffered(1))
    return pl.pallas_call(
        project_kernel,
        grid_spec=pltpu.PrefetchScalarGridSpec(
            num_scalar_prefetch=5,
            grid=(steps,),
            in_specs=[
                whole(xa.shape),
                whole(xb.shape),
                pl.BlockSpec((PER_STEP, ROWS, HALF), lambda s, *_: (jnp.minimum(s, half - 1), 0, 0)),
                pl.BlockSpec((PER_STEP, ROWS, HALF), lambda s, *_: (jnp.maximum(s - half, 0), 0, 0)),
            ],
            out_specs=pl.BlockSpec((rows, HALF), lambda s, *_: (0, 0)),
            scratch_shapes=[pltpu.VMEM((rows, HALF), jnp.float32)],
        ),
        out_shape=jax.ShapeDtypeStruct((rows, HALF), jnp.bfloat16),
        compiler_params=pltpu.CompilerParams(vmem_limit_bytes=48 * 1024 * 1024),
        cost_estimate=pl.CostEstimate(flops=2 * rows * 8192 * HALF, bytes_accessed=22_000_000, transcendentals=0),
        name="project",
    )(*tables, xa, xb, w1, w2)


def prefill_kernel(side_ref, mine_ref, other_ref, out_ref):
    first = side_ref[0] == 0
    mine, other = mine_ref[...], other_ref[...]
    low = jnp.where(first, mine, other)
    high = jnp.where(first, other, mine)
    keys, values = low[:, 512:], high[:, 512:]
    row = lax.broadcasted_iota(jnp.int32, (SEQ_LEN, SEQ_LEN), 0)
    col = lax.broadcasted_iota(jnp.int32, (SEQ_LEN, SEQ_LEN), 1)
    causal = row >= col
    for head in range(HEADS):
        part = low if head < 4 else high
        query = part[:, (head % 4) * HD : (head % 4 + 1) * HD]
        scores = lax.dot_general(query, keys, (((1,), (1,)), ((), ())), preferred_element_type=jnp.float32) * SCALE
        scores = jnp.where(causal, scores, negative_big)
        expos = jnp.exp(scores - jnp.max(scores, axis=-1, keepdims=True))
        sums = jnp.sum(expos, axis=-1, keepdims=True)
        weighted = jnp.dot(expos.astype(jnp.bfloat16), values, preferred_element_type=jnp.float32) / sums
        out_ref[:, head * HD : (head + 1) * HD] = weighted.astype(out_ref.dtype)


def prefill(side, mine, other):
    return pl.pallas_call(
        prefill_kernel,
        grid_spec=pltpu.PrefetchScalarGridSpec(
            num_scalar_prefetch=1,
            grid=(ROWS // SEQ_LEN,),
            in_specs=[pl.BlockSpec((SEQ_LEN, HALF), lambda s, *_: (s, 0))] * 2,
            out_specs=pl.BlockSpec((SEQ_LEN, WIDTH), lambda s, *_: (s, 0)),
        ),
        out_shape=jax.ShapeDtypeStruct((ROWS, WIDTH), jnp.bfloat16),
        cost_estimate=pl.CostEstimate(flops=70_000_000, bytes_accessed=1_200_000, transcendentals=262144),
        name="prefill_attention",
    )(side, mine, other)


def decode(side, mine, other, key_cache, value_cache, lengths, rep):
    low = jnp.where(side == 0, mine, other)
    high = jnp.where(side == 0, other, mine)
    queries = jnp.concatenate([low[:, :512].reshape(BATCH, 4, HD), high[:, :512].reshape(BATCH, 4, HD)], axis=1)
    own_key, own_value = low[:, 512:], high[:, 512:]
    positions_here = key_cache.shape[1]
    scores = jnp.einsum("bgd,bpd->bgp", queries, key_cache, preferred_element_type=jnp.float32) * SCALE
    position = rep * positions_here + jnp.arange(positions_here, dtype=jnp.int32)
    allowed = (position[None, :] < lengths[:, None])[:, None, :]
    own = jnp.einsum("bgd,bd->bg", queries, own_key, preferred_element_type=jnp.float32) * SCALE
    with_own = rep == 0
    own = jnp.where(with_own, own, negative_big)
    local_max = jnp.maximum(jnp.max(jnp.where(allowed, scores, negative_big), axis=-1), own)
    expos = jnp.where(allowed, jnp.exp(scores - local_max[..., None]), 0.0)
    own_exp = jnp.where(with_own, jnp.exp(own - local_max), 0.0)
    local_sum = jnp.sum(expos, axis=-1) + own_exp
    local_out = jnp.einsum(
        "bgp,bpd->bgd", expos.astype(jnp.bfloat16), value_cache, preferred_element_type=jnp.float32
    )
    local_out = local_out + own_exp.astype(jnp.bfloat16).astype(jnp.float32)[..., None] * own_value.astype(jnp.float32)[:, None, :]
    count = 32
    pairs = BATCH * HEADS // count
    stats = jnp.stack([local_max.reshape(count, pairs), local_sum.reshape(count, pairs)], axis=1)
    stats = jnp.pad(stats, ((0, 0), (0, 16 - pairs - 2), (0, HD - pairs)))
    packed = jnp.concatenate([local_out.reshape(count, pairs, HD), stats], axis=1)
    got = lax.all_to_all(packed, REP, 0, 0, tiled=True)
    tops, sums, outs = got[:, pairs, :pairs], got[:, pairs + 1, :pairs], got[:, :pairs]
    highest = jnp.max(tops, axis=0)
    keep = jnp.exp(tops - highest[None])
    numer = jnp.sum(outs * keep[:, :, None], axis=0)
    denom = jnp.sum(sums * keep, axis=0)
    done = jnp.pad((numer / denom[:, None]).astype(jnp.bfloat16), ((0, 16 - pairs), (0, 0)))
    every = lax.all_to_all(jnp.broadcast_to(done[None], (count, 16, HD)), REP, 0, 0, tiled=True)
    return every[:, :pairs].reshape(BATCH, HEADS * HD)


def per_device(prefill_x, decode_x, query_weight, keyvalue_weight, key_cache, value_cache, cache_lengths, chain_order):
    xl, z, c = lax.axis_index("xl"), lax.axis_index("z"), lax.axis_index("c")
    xh, y = lax.axis_index("xh"), lax.axis_index("y")
    x = xh * 2 + xl
    rep = xl * 16 + z * 2 + c

    first = jnp.concatenate([query_weight[:, :512], keyvalue_weight[:, :HD]], axis=1)
    second = jnp.concatenate([query_weight[:, 512:], keyvalue_weight[:, HD:]], axis=1)
    kept = jnp.where(xl == 0, first, second)
    given = jnp.where(xl == 0, second, first)
    w1 = lax.all_gather(kept, ("z", "c"))
    w2 = lax.all_gather(ring(given, "xl", 2, 1), ("z", "c"))

    top, low = prefill_x[:128], prefill_x[128:]
    decode_other = lax.ppermute(decode_x, X, [(flat_x(i), flat_x(3 - i)) for i in range(4)])
    xa = around(top, X, 64)
    xb = around(low, "y", 64)
    xa = around(jnp.concatenate([xa, decode_x, decode_other], axis=0), "y", 304).reshape(4, 608, WIDTH)
    xb = around(xb, X, 256).reshape(4, 512, WIDTH)

    near = xl * 16 + jnp.arange(16, dtype=jnp.int32)
    stored = jnp.concatenate([near, (near + 16) % 32])
    logical = jnp.sum(
        jnp.where(chain_order[None, :] == stored[:, None], jnp.arange(32, dtype=jnp.int32)[None, :], 0), axis=1
    )
    group = logical // 4
    from_xh, from_y = group // 4, group % 4
    tables = (
        logical % 4,
        slot_of(from_y, y),
        slot_of(2 * from_xh + 1 - xl, x),
        slot_of(2 * from_xh + xl, x),
        (from_xh != xh).astype(jnp.int32),
    )
    rows = project(tables, xa, xb, w1, w2)
    dec_mine = rows[ROWS : ROWS + BATCH]
    pre_mine = rows[ROWS + BATCH :]
    dec_other = ring(dec_mine, "xl", 2, 1)
    pre_other = ring(rows[:ROWS], "xl", 2, 1)
    attn_dec = decode(xl, dec_mine, dec_other, key_cache, value_cache, cache_lengths, rep)
    attn_pre = prefill(xl.reshape(1).astype(jnp.int32), pre_mine, pre_other)
    return attn_pre, attn_dec


def solution(mesh):
    fine = Mesh(np.asarray(mesh.devices).reshape(2, 8, 2, 2, 4), ("xl", "z", "c", "xh", "y"))
    rep, tp = REP, ("xh", "y")
    in_specs = (P(rep, tp), P(None, tp), P(rep, tp), P(rep, tp), P(None, rep, tp), P(None, rep, tp), P(), P())
    out_specs = (P(rep, tp), P(None, tp))
    return jax.shard_map(per_device, mesh=fine, in_specs=in_specs, out_specs=out_specs, check_vma=False)
```

time: 388 us -> 167 us (0.43)
  waiting for transfers between devices: 189 us -> 55.6 us
  blocking collectives: 96.4 us -> 0 us
  starting transfers between devices: 0.15 us -> 41.5 us
  other arithmetic: 42.8 us -> 2.63 us
  Pallas kernels: 0 us -> 19.3 us
  matrix products: 20.6 us -> 3.16 us
  local copies, waits for them, and re-layouts: 22.6 us -> 30.2 us
    all_gather x4 -> x2, waiting for transfers between devices: 187 us -> 14.9 us  [the longest x1 14.9 us: per_device(): w2 = lax.all_gather(ring(given, 'xl', 2, 1), ('z', 'c'))]
    all_gather x3 -> x0, blocking collectives: 96.4 us -> none  [the longest x2 64 us: combined_all(): everything = jax.tree.map(lambda part: lax.all_gather(part, axis), shard)]
    add x63 -> x1, other arithmetic: 36 us -> 0.01 us  [decode(): rep * positions_here + jnp.arange(positions_here, dtype=jnp.int32)]
    ppermute x0 -> x20, starting transfers between devices: none -> 29.6 us  [the longest x19 28.4 us: ring(): return lax.ppermute(value, axes, pairs)]
    ppermute x0 -> x20, waiting for transfers between devices: none -> 28.3 us  [the longest x19 28.3 us: ring(): return lax.ppermute(value, axes, pairs)]
    pallas_call x0 -> x2, Pallas kernels: none -> 19.3 us  [the longest x1 13.5 us: project(): pl.pallas_call(project_kernel, grid_spec=pltpu.PrefetchScalarGridSpec(num...]
    unnamed x13 -> x31, local copies, waits for them, and re-layouts: 1.84 us -> 20.1 us
    dot_general x7 -> x3, matrix products: 20.6 us -> 3.16 us  [the longest x1 1.99 us: decode(): jnp.einsum('bgp,bpd->bgd', expos.astype(jnp.bfloat16), value_cache, prefe...]
  transfers between devices with their start and end apart: 4 -> 24, of which waited for: 3 -> 9; matrix products, arithmetic and copies ran while one was open for 11% -> 14% of each run, Pallas kernels for 0% -> 3%
where the time goes in v1:
time: 167 us
  waiting for transfers between devices  55.6 us (33%)
  starting transfers between devices  41.5 us (25%)
  local copies, waits for them, and re-layouts  30.2 us (18%)
  Pallas kernels  19.3 us (12%)
  between operations  14.4 us (9%)
  matrix products  3.16 us (2%)
  other arithmetic  2.63 us (2%)
    ppermute x19, starting transfers between devices, ring(): return lax.ppermute(value, axes, pairs)  28.4 us
    ppermute x19, waiting for transfers between devices, ring(): return lax.ppermute(value, axes, pairs)  28.3 us
    unnamed x31, local copies, waits for them, and re-layouts  20.1 us
    all_gather x1, waiting for transfers between devices, per_device(): w2 = lax.all_gather(ring(given, 'xl', 2, 1), ('z', 'c'))  14.9 us
    pallas_call x1, Pallas kernels, project(): pl.pallas_call(project_kernel, grid_spec=pltpu.PrefetchScalarGridSpec(num...  13.5 us
    all_to_all x1, waiting for transfers between devices, decode(): got = lax.all_to_all(packed, REP, 0, 0, tiled=True)  9.73 us
    all_to_all x1, starting transfers between devices, decode(): got = lax.all_to_all(packed, REP, 0, 0, tiled=True)  6.8 us
    pallas_call x1, Pallas kernels, prefill(): pl.pallas_call(prefill_kernel, grid_spec=pltpu.PrefetchScalarGridSpec(num...  5.79 us
  transfers between devices with their start and end apart: 24, of which 9 were waited for; matrix products, arithmetic and copies ran while one was open for 14% of the time, Pallas kernels for 3%

profile of v1, /device:TPU:1, one launch (start us, length us, event | category | flops | bytes accessed | tf_op | source)
XLA Modules:
  0.0 166.7 jit_solution(2755522664051976303)
XLA Ops:
  7.3 1.2 fusion.23
  8.5 0.9 fusion.25
  10.4 2.1 %collective-permute-start.17 = (bf16[256,640]{1,0:T(8,128)(2,1)S(1)}, bf16[256,640]{1,0:T(8,128)(2,1)S(1)}, u32[]{:S(2)}, u32[]{:S(2)}) collective-permute-start(bf16[256,640]{1,0:T(8,128)(2,1)S(1)} %maximum_select_fusion.1), channel_id=1, source_target_pairs={{0,128},{128,0},{1,129},{129,1},{2,130},{130,2},{3,131},{131,3},{4... | collective-permute-start | bytes 983048 | tf_op jit(solution)/shard_map/ppermute | solution.py:35
  12.5 6.1 %collective-permute-done.17 = bf16[256,640]{1,0:T(8,128)(2,1)S(1)} collective-permute-done((bf16[256,640]{1,0:T(8,128)(2,1)S(1)}, bf16[256,640]{1,0:T(8,128)(2,1)S(1)}, u32[]{:S(2)}, u32[]{:S(2)}) %collective-permute-start.17) | collective-permute-done | bytes 327712 | tf_op jit(solution)/shard_map/ppermute | solution.py:35
  19.4 1.2 constant_dynamic-update-slice_fusion.22
  20.6 2.6 %collective-permute-start.9 = (bf16[128,1024]{1,0:T(8,128)(2,1)}, bf16[128,1024]{1,0:T(8,128)(2,1)S(1)}, u32[]{:S(2)}, u32[]{:S(2)}) collective-permute-start(bf16[128,1024]{1,0:T(8,128)(2,1)} %get-tuple-element.19), channel_id=1, source_target_pairs={{0,1},{1,2},{2,3},{3,0},{4,5},{5,6},{6,7},{7,4},{8,9},{9,10},{10,1... | collective-permute-start | bytes 786440 | tf_op jit(solution)/shard_map/ppermute | solution.py:35
  23.2 1.4 collective-permute-start.10
  24.6 1.2 collective-permute-start
  25.9 1.5 collective-permute-start.1
  27.3 1.3 collective-permute-start.4
  28.7 1.3 collective-permute-done.9
  30.2 2.7 %collective-permute-start.12 = (bf16[64,1024]{1,0:T(8,128)(2,1)S(1)}, bf16[64,1024]{1,0:T(8,128)(2,1)S(1)}, u32[]{:S(2)}, u32[]{:S(2)}) collective-permute-start(bf16[64,1024]{1,0:T(8,128)(2,1)S(1)} %slice.105), channel_id=1, source_target_pairs={{0,3},{1,0},{2,1},{3,2},{4,7},{5,4},{6,5},{7,6},{8,11},{9,8},{10,9... | collective-permute-start | bytes 393224 | tf_op jit(solution)/shard_map/ppermute | solution.py:35
  32.9 1.0 collective-permute-start.2
  33.9 1.9 %collective-permute-start.3 = (bf16[64,1024]{1,0:T(8,128)(2,1)S(1)}, bf16[64,1024]{1,0:T(8,128)(2,1)S(1)}, u32[]{:S(2)}, u32[]{:S(2)}) collective-permute-start(bf16[64,1024]{1,0:T(8,128)(2,1)S(1)} %slice.101), channel_id=1, source_target_pairs={{0,132},{128,0},{4,128},{132,4},{1,133},{129,1},{5,129},{133,5},{2... | collective-permute-start | bytes 393224 | tf_op jit(solution)/shard_map/ppermute | solution.py:35
  35.7 0.9 constant_dynamic-update-slice_fusion.21
  36.6 0.9 constant_dynamic-update-slice_fusion.20
  37.5 0.9 constant_dynamic-update-slice_fusion.5
  38.4 0.9 constant_dynamic-update-slice_fusion.4
  40.7 2.7 %collective-permute-start.14 = (bf16[512,1024]{1,0:T(8,128)(2,1)}, bf16[512,1024]{1,0:T(8,128)(2,1)}, u32[]{:S(2)}, u32[]{:S(2)}) collective-permute-start(bf16[512,1024]{1,0:T(8,128)(2,1)} %get-tuple-element.35), channel_id=1, source_target_pairs={{0,132},{128,0},{4,128},{132,4},{1,133},{129,1},{5,129},{133,5},{2... | collective-permute-start | bytes 3145736 | tf_op jit(solution)/shard_map/ppermute | solution.py:35
  46.5 2.8 %collective-permute-start.6 = (bf16[608,1024]{1,0:T(8,128)(2,1)}, bf16[608,1024]{1,0:T(8,128)(2,1)S(1)}, u32[]{:S(2)}, u32[]{:S(2)}) collective-permute-start(bf16[608,1024]{1,0:T(8,128)(2,1)} %get-tuple-element.43), channel_id=1, source_target_pairs={{0,3},{1,0},{2,1},{3,2},{4,7},{5,4},{6,5},{7,6},{8,11},{9,8},{10,9... | collective-permute-start | bytes 3735560 | tf_op jit(solution)/shard_map/ppermute | solution.py:35
  49.3 14.3 %collective-permute-done.13 = bf16[512,1024]{1,0:T(8,128)(2,1)} collective-permute-done((bf16[512,1024]{1,0:T(8,128)(2,1)}, bf16[512,1024]{1,0:T(8,128)(2,1)}, u32[]{:S(2)}, u32[]{:S(2)}) %collective-permute-start.13) | collective-permute-done | bytes 1048608 | tf_op jit(solution)/shard_map/ppermute | solution.py:35
  63.6 1.1 slice.106
  65.0 1.1 slice.107
  66.0 2.7 %collective-permute-start.16 = (bf16[256,1024]{1,0:T(8,128)(2,1)S(1)}, bf16[256,1024]{1,0:T(8,128)(2,1)S(1)}, u32[]{:S(2)}, u32[]{:S(2)}) collective-permute-start(bf16[256,1024]{1,0:T(8,128)(2,1)S(1)} %slice.107), channel_id=1, source_target_pairs={{0,132},{128,0},{4,128},{132,4},{1,133},{129,1},{5,129},{133,5},{2... | collective-permute-start | bytes 1572872 | tf_op jit(solution)/shard_map/ppermute | solution.py:35
  68.8 2.5 %constant_dynamic-update-slice_fusion.26 = bf16[2048,1024]{1,0:T(8,128)(2,1)} fusion(bf16[2048,1024]{1,0:T(8,128)(2,1)} %get-tuple-element.36, bf16[512,1024]{1,0:T(8,128)(2,1)} %collective-permute-done.13), kind=kLoop, calls=%fused_computation.42 | loop fusion | bytes 2097152
  71.3 1.4 collective-permute-done.5
  72.8 2.3 %constant_dynamic-update-slice_fusion.25 = bf16[2048,1024]{1,0:T(8,128)(2,1)} fusion(bf16[2048,1024]{1,0:T(8,128)(2,1)} %constant_dynamic-update-slice_fusion.26, bf16[512,1024]{1,0:T(8,128)(2,1)} %collective-permute-done.14), kind=kLoop, calls=%fused_computation.41 | loop fusion | bytes 2097152
  75.1 2.7 %collective-permute-start.8 = (bf16[304,1024]{1,0:T(8,128)(2,1)S(1)}, bf16[304,1024]{1,0:T(8,128)(2,1)S(1)}, u32[]{:S(2)}, u32[]{:S(2)}) collective-permute-start(bf16[304,1024]{1,0:T(8,128)(2,1)S(1)} %slice.103), channel_id=1, source_target_pairs={{0,3},{1,0},{2,1},{3,2},{4,7},{5,4},{6,5},{7,6},{8,11},{9,8},{10,9... | collective-permute-start | bytes 1867784 | tf_op jit(solution)/shard_map/ppermute | solution.py:35
  77.9 1.2 constant_dynamic-update-slice_fusion.10
  79.1 1.1 constant_dynamic-update-slice_fusion.9
  80.2 0.8 constant_dynamic-update-slice_fusion.24
  81.1 0.8 constant_dynamic-update-slice_fusion.23
  81.9 3.3 %collective-permute-done.7 = bf16[304,1024]{1,0:T(8,128)(2,1)S(1)} collective-permute-done((bf16[304,1024]{1,0:T(8,128)(2,1)S(1)}, bf16[304,1024]{1,0:T(8,128)(2,1)S(1)}, u32[]{:S(2)}, u32[]{:S(2)}) %collective-permute-start.7) | collective-permute-done | bytes 622624 | tf_op jit(solution)/shard_map/ppermute | solution.py:35
  85.2 0.9 constant_dynamic-update-slice_fusion.8
  86.1 0.9 constant_dynamic-update-slice_fusion.7
  87.0 14.9 %all-gather.6.cloned.1.call-done = bf16[4096,640]{1,0:T(8,128)(2,1)} async-done(((bf16[256,640]{1,0:T(8,128)(2,1)}), bf16[4096,640]{1,0:T(8,128)(2,1)}) %all-gather.6.cloned.1.call-update) | async-done | bytes 5242896 | tf_op jit(solution)/shard_map/all_gather | solution.py:204
  101.9 2.2 %copy-done.1 = bf16[2048,1024]{1,0:T(8,128)(2,1)S(1)} copy-done((bf16[2048,1024]{1,0:T(8,128)(2,1)S(1)}, bf16[2048,1024]{1,0:T(8,128)(2,1)}, u32[]{:S(2)}) %copy-start.1) | copy-done | bytes 4194328
  104.0 13.5 %project.1 = bf16[560,640]{1,0:T(8,128)(2,1)S(1)} custom-call(s32[32]{0:T(128)S(1)} %and_select_fusion.6.col_ref, s32[32]{0:T(128)S(1)} %compare_select_fusion.16.sy_ref, s32[32]{0:T(128)S(1)} %get-tuple-element.50.sp_ref, s32[32]{0:T(128)S(1)} %get-tuple-element.49.so_ref, s32[32]{0:T(128)S(1)} %get-tuple-element.4.sd_ref, ...), custom_call_target="tpu_custom_call" | custom-call | flops 5872025600 | bytes 22000000 | tf_op jit(solution)/shard_map/project/pallas_call | solution.py:101
  117.5 1.2 collective-permute-start.19
  118.9 1.8 %collective-permute-done.19 = bf16[48,640]{1,0:T(8,128)(2,1)S(1)} collective-permute-done((bf16[48,640]{1,0:T(8,128)(2,1)S(1)}, bf16[48,640]{1,0:T(8,128)(2,1)S(1)}, u32[]{:S(2)}, u32[]{:S(2)}) %collective-permute-start.19) | collective-permute-done | bytes 61472 | tf_op jit(solution)/shard_map/ppermute | solution.py:35
  121.0 1.0 select_reduce_fusion
  122.3 2.0 %multiply_add_fusion = f32[48,8,128]{2,1,0:T(8,128)S(1)} fusion(f32[48,128]{1,0:T(8,128)S(1)} %slice_convert_fusion, f32[48,8]{1,0:T(8,128)S(1)} %get-tuple-element.47, bf16[48,128,128]{2,1,0:T(8,128)(2,1)} %param.13, f32[48,8,128]{2,1,0:T(8,128)S(1)} %get-tuple-element.52, f32[48,8]{1,0:T(8,128)S(1)} %fusion.12, pred[48,128]{1,0:T(8,128)(4,1)S(1)} %broadcast_compare_fusion), kind=kOutput, calls=%fused_computation.6 | convolution fusion | flops 12828672 | bytes 1999872 | tf_op jit(solution)/shard_map/bgp,bpd->bgd/dot_general | solution.py:173
  125.2 6.8 %all-to-all-start = ((f32[32,16,128]{2,1,0:T(8,128)}), f32[32,16,128]{2,1,0:T(8,128)S(1)}, u32[]{:S(2)}, u32[]{:S(2)}) async-start(f32[32,16,128]{2,1,0:T(8,128)} %pad_maximum_fusion), calls=%async_computation | async-start | bytes 524288 | tf_op jit(solution)/shard_map/all_to_all | solution.py:182
  132.8 1.4 collective-permute-start.18
  134.2 9.7 %all-to-all-done = f32[32,16,128]{2,1,0:T(8,128)S(1)} async-done(((f32[32,16,128]{2,1,0:T(8,128)}), f32[32,16,128]{2,1,0:T(8,128)S(1)}, u32[]{:S(2)}, u32[]{:S(2)}) %all-to-all-start) | async-done | bytes 262176 | tf_op jit(solution)/shard_map/all_to_all | solution.py:182
  145.0 5.0 %all-to-all-start.1 = ((bf16[32,16,128]{2,1,0:T(8,128)(2,1)}), bf16[32,16,128]{2,1,0:T(8,128)(2,1)S(1)}, u32[]{:S(2)}, u32[]{:S(2)}) async-start(bf16[32,16,128]{2,1,0:T(8,128)(2,1)} %broadcast_in_dim.77), calls=%async_computation.1 | async-start | bytes 262144 | tf_op jit(solution)/shard_map/all_to_all | solution.py:189
  150.7 5.8 %prefill_attention.1 = bf16[256,1024]{1,0:T(8,128)(2,1)} custom-call(s32[1]{0:T(128)} %bitcast.side_ref, bf16[256,640]{1,0:T(8,128)(2,1)} %get-tuple-element.10.mine_ref, bf16[256,640]{1,0:T(8,128)(2,1)} %copy-done.4), custom_call_target="tpu_custom_call" | custom-call | flops 70000000 | bytes 1200000 | tf_op jit(solution)/shard_map/prefill_attention/pallas_call | solution.py:143
  156.5 2.6 %all-to-all-done.1 = bf16[32,16,128]{2,1,0:T(8,128)(2,1)S(1)} async-done(((bf16[32,16,128]{2,1,0:T(8,128)(2,1)}), bf16[32,16,128]{2,1,0:T(8,128)(2,1)S(1)}, u32[]{:S(2)}, u32[]{:S(2)}) %all-to-all-start.1) | async-done | bytes 131104 | tf_op jit(solution)/shard_map/all_to_all | solution.py:189
  (88 shorter events, 11.9 us)
Async XLA Ops:
  7.2 113.8 %copy-start = (bf16[48,128,128]{2,1,0:T(8,128)(2,1)S(1)}, bf16[48,128,128]{2,1,0:T(8,128)(2,1)}, u32[]{:S(2)}) copy-start(bf16[48,128,128]{2,1,0:T(8,128)(2,1)} %param.12) | copy-start | bytes 4718596
  7.2 12.2 %copy-start.2 = (bf16[256,1024]{1,0:T(8,128)(2,1)S(1)}, bf16[256,1024]{1,0:T(8,128)(2,1)}, u32[]{:S(2)}) copy-start(bf16[256,1024]{1,0:T(8,128)(2,1)} %param.8) | copy-start | bytes 1572868
  7.2 20.1 %copy-start.5 = (bf16[48,1024]{1,0:T(8,128)(2,1)S(1)}, bf16[48,1024]{1,0:T(8,128)(2,1)}, u32[]{:S(2)}) copy-start(bf16[48,1024]{1,0:T(8,128)(2,1)} %param.9) | copy-start | bytes 294916
  7.2 79.8 %all-gather.4.cloned.1.call-start = ((), (), s32[]{:S(2)}) async-start(), calls=%async_computation.2 | async-start | bytes 5570560 | tf_op jit(solution)/shard_map/all_gather | solution.py:203
  10.3 91.6 %all-gather.6.cloned.1.call-start = ((), (), s32[]{:S(2)}) async-start(), calls=%async_computation.3 | async-start | bytes 5570560 | tf_op jit(solution)/shard_map/all_gather | solution.py:204
  10.4 8.2 %collective-permute-start.17 = (bf16[256,640]{1,0:T(8,128)(2,1)S(1)}, bf16[256,640]{1,0:T(8,128)(2,1)S(1)}, u32[]{:S(2)}, u32[]{:S(2)}) collective-permute-start(bf16[256,640]{1,0:T(8,128)(2,1)S(1)} %maximum_select_fusion.1), channel_id=1, source_target_pairs={{0,128},{128,0},{1,129},{129,1},{2,130},{130,2},{3,131},{131,3},{4... | collective-permute-start | bytes 983048 | tf_op jit(solution)/shard_map/ppermute | solution.py:35
  18.6 0.7 copy-start.3
  19.4 26.9 %copy-start.7 = (s32[32]{0:T(128)S(1)}, s32[32]{0:T(128)}, u32[]{:S(2)}) copy-start(s32[32]{0:T(128)} %param.15) | copy-start | bytes 388
  20.6 9.4 %collective-permute-start.9 = (bf16[128,1024]{1,0:T(8,128)(2,1)}, bf16[128,1024]{1,0:T(8,128)(2,1)S(1)}, u32[]{:S(2)}, u32[]{:S(2)}) collective-permute-start(bf16[128,1024]{1,0:T(8,128)(2,1)} %get-tuple-element.19), channel_id=1, source_target_pairs={{0,1},{1,2},{2,3},{3,0},{4,5},{5,6},{6,7},{7,4},{8,9},{9,10},{10,1... | collective-permute-start | bytes 786440 | tf_op jit(solution)/shard_map/ppermute | solution.py:35
  23.2 6.9 %collective-permute-start.10 = (bf16[128,1024]{1,0:T(8,128)(2,1)}, bf16[128,1024]{1,0:T(8,128)(2,1)S(1)}, u32[]{:S(2)}, u32[]{:S(2)}) collective-permute-start(bf16[128,1024]{1,0:T(8,128)(2,1)} %get-tuple-element.19), channel_id=1, source_target_pairs={{0,3},{1,0},{2,1},{3,2},{4,7},{5,4},{6,5},{7,6},{8,11},{9,8},{10,9... | collective-permute-start | bytes 786440 | tf_op jit(solution)/shard_map/ppermute | solution.py:35
  24.6 8.2 %collective-permute-start = (bf16[128,1024]{1,0:T(8,128)(2,1)S(1)}, bf16[128,1024]{1,0:T(8,128)(2,1)S(1)}, u32[]{:S(2)}, u32[]{:S(2)}) collective-permute-start(bf16[128,1024]{1,0:T(8,128)(2,1)S(1)} %get-tuple-element.20), channel_id=1, source_target_pairs={{0,128},{128,4},{4,132},{132,0},{1,129},{129,5},{5,133},{133,1},{2... | collective-permute-start | bytes 786440 | tf_op jit(solution)/shard_map/ppermute | solution.py:35
  25.9 8.0 %collective-permute-start.1 = (bf16[128,1024]{1,0:T(8,128)(2,1)S(1)}, bf16[128,1024]{1,0:T(8,128)(2,1)S(1)}, u32[]{:S(2)}, u32[]{:S(2)}) collective-permute-start(bf16[128,1024]{1,0:T(8,128)(2,1)S(1)} %get-tuple-element.20), channel_id=1, source_target_pairs={{0,132},{128,0},{4,128},{132,4},{1,133},{129,1},{5,129},{133,5},{2... | collective-permute-start | bytes 786440 | tf_op jit(solution)/shard_map/ppermute | solution.py:35
  27.3 18.2 %collective-permute-start.4 = (bf16[48,1024]{1,0:T(8,128)(2,1)S(1)}, bf16[48,1024]{1,0:T(8,128)(2,1)S(1)}, u32[]{:S(2)}, u32[]{:S(2)}) collective-permute-start(bf16[48,1024]{1,0:T(8,128)(2,1)S(1)} %copy-done.5), channel_id=1, source_target_pairs={{0,132},{128,4},{4,128},{132,0},{1,133},{129,5},{5,129},{133,1},{2... | collective-permute-start | bytes 294920 | tf_op jit(solution)/shard_map/ppermute | solution.py:207
  30.0 9.2 %collective-permute-start.11 = (bf16[64,1024]{1,0:T(8,128)(2,1)S(1)}, bf16[64,1024]{1,0:T(8,128)(2,1)S(1)}, u32[]{:S(2)}, u32[]{:S(2)}) collective-permute-start(bf16[64,1024]{1,0:T(8,128)(2,1)S(1)} %slice.104), channel_id=1, source_target_pairs={{0,1},{1,2},{2,3},{3,0},{4,5},{5,6},{6,7},{7,4},{8,9},{9,10},{10,1... | collective-permute-start | bytes 393224 | tf_op jit(solution)/shard_map/ppermute | solution.py:35
  30.2 9.8 %collective-permute-start.12 = (bf16[64,1024]{1,0:T(8,128)(2,1)S(1)}, bf16[64,1024]{1,0:T(8,128)(2,1)S(1)}, u32[]{:S(2)}, u32[]{:S(2)}) collective-permute-start(bf16[64,1024]{1,0:T(8,128)(2,1)S(1)} %slice.105), channel_id=1, source_target_pairs={{0,3},{1,0},{2,1},{3,2},{4,7},{5,4},{6,5},{7,6},{8,11},{9,8},{10,9... | collective-permute-start | bytes 393224 | tf_op jit(solution)/shard_map/ppermute | solution.py:35
  32.9 10.5 %collective-permute-start.2 = (bf16[64,1024]{1,0:T(8,128)(2,1)S(1)}, bf16[64,1024]{1,0:T(8,128)(2,1)S(1)}, u32[]{:S(2)}, u32[]{:S(2)}) collective-permute-start(bf16[64,1024]{1,0:T(8,128)(2,1)S(1)} %slice.100), channel_id=1, source_target_pairs={{0,128},{128,4},{4,132},{132,0},{1,129},{129,5},{5,133},{133,1},{2... | collective-permute-start | bytes 393224 | tf_op jit(solution)/shard_map/ppermute | solution.py:35
  33.9 10.3 %collective-permute-start.3 = (bf16[64,1024]{1,0:T(8,128)(2,1)S(1)}, bf16[64,1024]{1,0:T(8,128)(2,1)S(1)}, u32[]{:S(2)}, u32[]{:S(2)}) collective-permute-start(bf16[64,1024]{1,0:T(8,128)(2,1)S(1)} %slice.101), channel_id=1, source_target_pairs={{0,132},{128,0},{4,128},{132,4},{1,133},{129,1},{5,129},{133,5},{2... | collective-permute-start | bytes 393224 | tf_op jit(solution)/shard_map/ppermute | solution.py:35
  40.7 22.9 %collective-permute-start.13 = (bf16[512,1024]{1,0:T(8,128)(2,1)}, bf16[512,1024]{1,0:T(8,128)(2,1)}, u32[]{:S(2)}, u32[]{:S(2)}) collective-permute-start(bf16[512,1024]{1,0:T(8,128)(2,1)} %get-tuple-element.35), channel_id=1, source_target_pairs={{0,128},{128,4},{4,132},{132,0},{1,129},{129,5},{5,133},{133,1},{2... | collective-permute-start | bytes 3145736 | tf_op jit(solution)/shard_map/ppermute | solution.py:35
  40.7 24.2 %collective-permute-start.14 = (bf16[512,1024]{1,0:T(8,128)(2,1)}, bf16[512,1024]{1,0:T(8,128)(2,1)}, u32[]{:S(2)}, u32[]{:S(2)}) collective-permute-start(bf16[512,1024]{1,0:T(8,128)(2,1)} %get-tuple-element.35), channel_id=1, source_target_pairs={{0,132},{128,0},{4,128},{132,4},{1,133},{129,1},{5,129},{133,5},{2... | collective-permute-start | bytes 3145736 | tf_op jit(solution)/shard_map/ppermute | solution.py:35
  46.3 26.4 %collective-permute-start.5 = (bf16[608,1024]{1,0:T(8,128)(2,1)}, bf16[608,1024]{1,0:T(8,128)(2,1)S(1)}, u32[]{:S(2)}, u32[]{:S(2)}) collective-permute-start(bf16[608,1024]{1,0:T(8,128)(2,1)} %get-tuple-element.43), channel_id=1, source_target_pairs={{0,1},{1,2},{2,3},{3,0},{4,5},{5,6},{6,7},{7,4},{8,9},{9,10},{10,1... | collective-permute-start | bytes 3735560 | tf_op jit(solution)/shard_map/ppermute | solution.py:35
  46.5 28.6 %collective-permute-start.6 = (bf16[608,1024]{1,0:T(8,128)(2,1)}, bf16[608,1024]{1,0:T(8,128)(2,1)S(1)}, u32[]{:S(2)}, u32[]{:S(2)}) collective-permute-start(bf16[608,1024]{1,0:T(8,128)(2,1)} %get-tuple-element.43), channel_id=1, source_target_pairs={{0,3},{1,0},{2,1},{3,2},{4,7},{5,4},{6,5},{7,6},{8,11},{9,8},{10,9... | collective-permute-start | bytes 3735560 | tf_op jit(solution)/shard_map/ppermute | solution.py:35
  64.7 15.6 %collective-permute-start.15 = (bf16[256,1024]{1,0:T(8,128)(2,1)S(1)}, bf16[256,1024]{1,0:T(8,128)(2,1)S(1)}, u32[]{:S(2)}, u32[]{:S(2)}) collective-permute-start(bf16[256,1024]{1,0:T(8,128)(2,1)S(1)} %slice.106), channel_id=1, source_target_pairs={{0,128},{128,4},{4,132},{132,0},{1,129},{129,5},{5,133},{133,1},{2... | collective-permute-start | bytes 1572872 | tf_op jit(solution)/shard_map/ppermute | solution.py:35
  66.0 15.0 %collective-permute-start.16 = (bf16[256,1024]{1,0:T(8,128)(2,1)S(1)}, bf16[256,1024]{1,0:T(8,128)(2,1)S(1)}, u32[]{:S(2)}, u32[]{:S(2)}) collective-permute-start(bf16[256,1024]{1,0:T(8,128)(2,1)S(1)} %slice.107), channel_id=1, source_target_pairs={{0,132},{128,0},{4,128},{132,4},{1,133},{129,1},{5,129},{133,5},{2... | collective-permute-start | bytes 1572872 | tf_op jit(solution)/shard_map/ppermute | solution.py:35
  72.7 12.4 %collective-permute-start.7 = (bf16[304,1024]{1,0:T(8,128)(2,1)S(1)}, bf16[304,1024]{1,0:T(8,128)(2,1)S(1)}, u32[]{:S(2)}, u32[]{:S(2)}) collective-permute-start(bf16[304,1024]{1,0:T(8,128)(2,1)S(1)} %slice.102), channel_id=1, source_target_pairs={{0,1},{1,2},{2,3},{3,0},{4,5},{5,6},{6,7},{7,4},{8,9},{9,10},{10,1... | collective-permute-start | bytes 1867784 | tf_op jit(solution)/shard_map/ppermute | solution.py:35
  75.1 10.9 %collective-permute-start.8 = (bf16[304,1024]{1,0:T(8,128)(2,1)S(1)}, bf16[304,1024]{1,0:T(8,128)(2,1)S(1)}, u32[]{:S(2)}, u32[]{:S(2)}) collective-permute-start(bf16[304,1024]{1,0:T(8,128)(2,1)S(1)} %slice.103), channel_id=1, source_target_pairs={{0,3},{1,0},{2,1},{3,2},{4,7},{5,4},{6,5},{7,6},{8,11},{9,8},{10,9... | collective-permute-start | bytes 1867784 | tf_op jit(solution)/shard_map/ppermute | solution.py:35
  101.8 2.2 %copy-start.1 = (bf16[2048,1024]{1,0:T(8,128)(2,1)S(1)}, bf16[2048,1024]{1,0:T(8,128)(2,1)}, u32[]{:S(2)}) copy-start(bf16[2048,1024]{1,0:T(8,128)(2,1)} %constant_dynamic-update-slice_fusion.23) | copy-start | bytes 12582916
  104.0 14.7 %copy-start.6 = (s32[48]{0:T(128)S(1)}, s32[48]{0:T(128)}, u32[]{:S(2)}) copy-start(s32[48]{0:T(128)} %param.14) | copy-start | bytes 580
  117.5 3.2 %collective-permute-start.19 = (bf16[48,640]{1,0:T(8,128)(2,1)S(1)}, bf16[48,640]{1,0:T(8,128)(2,1)S(1)}, u32[]{:S(2)}, u32[]{:S(2)}) collective-permute-start(bf16[48,640]{1,0:T(8,128)(2,1)S(1)} %slice.110), channel_id=1, source_target_pairs={{0,128},{128,0},{1,129},{129,1},{2,130},{130,2},{3,131},{131,3},{4... | collective-permute-start | bytes 184328 | tf_op jit(solution)/shard_map/ppermute | solution.py:35
  125.2 18.7 %all-to-all-start = ((f32[32,16,128]{2,1,0:T(8,128)}), f32[32,16,128]{2,1,0:T(8,128)S(1)}, u32[]{:S(2)}, u32[]{:S(2)}) async-start(f32[32,16,128]{2,1,0:T(8,128)} %pad_maximum_fusion), calls=%async_computation | async-start | bytes 524288 | tf_op jit(solution)/shard_map/all_to_all | solution.py:182
  132.8 17.1 %collective-permute-start.18 = (bf16[256,640]{1,0:T(8,128)(2,1)S(1)}, bf16[256,640]{1,0:T(8,128)(2,1)S(1)}, u32[]{:S(2)}, u32[]{:S(2)}) collective-permute-start(bf16[256,640]{1,0:T(8,128)(2,1)S(1)} %get-tuple-element.9), channel_id=1, source_target_pairs={{0,128},{128,0},{1,129},{129,1},{2,130},{130,2},{3,131},{131,3},{4... | collective-permute-start | bytes 983048 | tf_op jit(solution)/shard_map/ppermute | solution.py:35
  145.0 14.2 %all-to-all-start.1 = ((bf16[32,16,128]{2,1,0:T(8,128)(2,1)}), bf16[32,16,128]{2,1,0:T(8,128)(2,1)S(1)}, u32[]{:S(2)}, u32[]{:S(2)}) async-start(bf16[32,16,128]{2,1,0:T(8,128)(2,1)} %broadcast_in_dim.77), calls=%async_computation.1 | async-start | bytes 262144 | tf_op jit(solution)/shard_map/all_to_all | solution.py:189
  150.0 0.7 copy-start.4
Sparse Core Ops, SparseCore 0:
  10.4 47.5 all-gather.3
  59.9 41.9 all-gather.5

commit v2 on v1

v2 whole, which is shorter than its diff:
```python
import functools
import math

import jax
import jax.numpy as jnp
import numpy as np
from jax import lax
from jax.experimental import pallas as pl
from jax.experimental.pallas import tpu as pltpu
from jax.sharding import Mesh
from jax.sharding import PartitionSpec as P

HD = 128
SEQ_LEN = 128
HEADS = 8
BATCH = 48
ROWS = 256
WIDTH = 1024
HALF = 640
COUNT = 32
SCALE = 1.0 / math.sqrt(HD)
REP = ("xl", "z", "c")
X = ("xl", "xh")
STEPS = (0, 3, 1, 2)
OWN, PARTNER = (0, 3), (1, 2)
negative_big = -1e30
f32 = jnp.float32


def flat_x(x):
    return (x % 2) * 2 + x // 2


def ring(value, axes, size, shift):
    pairs = [(i, (i + shift) % size) for i in range(size)]
    if axes == X:
        pairs = [(flat_x(i), flat_x(j)) for i, j in pairs]
    return lax.ppermute(value, axes, pairs)


def around(value, axes):
    return [value, ring(value, axes, 4, 1), ring(value, axes, 4, -1), ring(value, axes, 4, 2)]


def vmem(count):
    return [pl.BlockSpec(memory_space=pltpu.VMEM)] * count


def smem(count):
    return [pl.BlockSpec(memory_space=pltpu.SMEM)] * count


def anywhere(count):
    return [pl.BlockSpec(memory_space=pl.ANY)] * count


def params(mebibytes=12):
    return pltpu.CompilerParams(vmem_limit_bytes=mebibytes * 1024 * 1024)


def shaped(dtype, *shape):
    return jax.ShapeDtypeStruct(shape, dtype)


bf16 = functools.partial(shaped, jnp.bfloat16)


def split_kernel(place_ref, qw_ref, kv_ref, kept_ref, given_ref, sems):
    def write(left_ref, right_ref):
        copies = [
            pltpu.make_async_copy(qw_ref.at[:, :512], left_ref.at[:, :512], sems.at[0]),
            pltpu.make_async_copy(kv_ref.at[:, :HD], left_ref.at[:, 512:], sems.at[1]),
            pltpu.make_async_copy(qw_ref.at[:, 512:], right_ref.at[:, :512], sems.at[2]),
            pltpu.make_async_copy(kv_ref.at[:, HD:], right_ref.at[:, 512:], sems.at[3]),
        ]
        for copy in copies:
            copy.start()
        for copy in copies:
            copy.wait()

    @pl.when(place_ref[0] == 0)
    def _():
        write(kept_ref, given_ref)

    @pl.when(place_ref[0] != 0)
    def _():
        write(given_ref, kept_ref)


def split(place, qw, kv):
    return pl.pallas_call(
        split_kernel,
        in_specs=smem(1) + anywhere(2),
        out_specs=anywhere(2),
        out_shape=[bf16(ROWS, HALF)] * 2,
        scratch_shapes=[pltpu.SemaphoreType.DMA((4,))],
        compiler_params=params(),
        name="split",
    )(place, qw, kv)


def pack_kernel(*refs):
    row = 0
    for ref in refs[:-1]:
        refs[-1][row : row + ref.shape[0]] = ref[...]
        row += ref.shape[0]


def pack(parts):
    return pl.pallas_call(
        pack_kernel,
        in_specs=vmem(len(parts)),
        out_specs=pl.BlockSpec(memory_space=pltpu.VMEM),
        out_shape=bf16(sum(v.shape[0] for v in parts), parts[0].shape[1]),
        compiler_params=params(),
        name="pack",
    )(*parts)


def project_kernel(place_ref, logical_ref, *refs):
    a_refs, b_refs, w_ref, theirs_ref, mine_ref = refs[:4], refs[4:8], refs[8], refs[9], refs[10]
    x_all, w_all, acc, x_sem, w_sem = refs[11:]
    x, y = place_ref[1], place_ref[2]
    moves = []
    for i in range(4):
        for k in range(4):
            base = ROWS if k in OWN else 0
            group = (((x + STEPS[k]) % 4) // 2) * 4 + (y + STEPS[i]) % 4
            moves.append((a_refs[i].at[k * 128 : (k + 1) * 128], x_all.at[group, base : base + 128]))
            base = (ROWS if i in OWN else 0) + 128
            group = (((x + STEPS[i]) % 4) // 2) * 4 + (y + STEPS[k]) % 4
            moves.append((b_refs[i].at[k * 128 : (k + 1) * 128], x_all.at[group, base : base + 128]))
    moves = [pltpu.make_async_copy(src, dst, x_sem.at[n]) for n, (src, dst) in enumerate(moves)]
    loads = [pltpu.make_async_copy(w_ref.at[i], w_all.at[i], w_sem.at[i]) for i in range(8)]
    for copy in moves + loads:
        copy.start()
    for copy in moves:
        copy.wait()
    for i in range(8):
        loads[i].wait()
        lhs = []
        for k in range(4):
            block = logical_ref[4 * i + k]
            lhs.append(x_all[block // 4, :, pl.ds(pl.multiple_of((block % 4) * ROWS, ROWS), ROWS)])
        part = jnp.dot(jnp.concatenate(lhs, axis=1), w_all[i], preferred_element_type=f32)
        if i == 0:
            acc[...] = part
        elif i < 7:
            acc[...] += part
        else:
            done = (acc[...] + part).astype(jnp.bfloat16)
            theirs_ref[...] = done[:ROWS]
            mine_ref[...] = done[ROWS:]


def project(place, logical, a, b, w):
    rows = 2 * ROWS
    return pl.pallas_call(
        project_kernel,
        in_specs=smem(2) + anywhere(9),
        out_specs=vmem(2),
        out_shape=[bf16(ROWS, HALF)] * 2,
        scratch_shapes=[
            pltpu.VMEM((8, rows, WIDTH), jnp.bfloat16),
            pltpu.VMEM((8, 4 * ROWS, HALF), jnp.bfloat16),
            pltpu.VMEM((rows, HALF), f32),
            pltpu.SemaphoreType.DMA((32,)),
            pltpu.SemaphoreType.DMA((8,)),
        ],
        compiler_params=params(48),
        cost_estimate=pl.CostEstimate(flops=2 * rows * 8192 * HALF, bytes_accessed=19_000_000, transcendentals=0),
        name="project",
    )(place, logical, *a, *b, w)


def prefill_kernel(place_ref, mine_ref, other_ref, out_ref):
    first = place_ref[0] == 0
    mine, other = mine_ref[...], other_ref[...]
    low = jnp.where(first, mine, other)
    high = jnp.where(first, other, mine)
    row = lax.broadcasted_iota(jnp.int32, (SEQ_LEN, SEQ_LEN), 0)
    col = lax.broadcasted_iota(jnp.int32, (SEQ_LEN, SEQ_LEN), 1)
    causal = row >= col
    causal = jnp.concatenate([causal] * HEADS, axis=0)
    for n in range(ROWS // SEQ_LEN):
        at = slice(n * SEQ_LEN, (n + 1) * SEQ_LEN)
        keys, values = low[at, 512:], high[at, 512:]
        queries = [part[at, h * HD : (h + 1) * HD] for part in (low, high) for h in range(4)]
        scores = lax.dot_general(
            jnp.concatenate(queries, axis=0), keys, (((1,), (1,)), ((), ())), preferred_element_type=f32
        ) * SCALE
        scores = jnp.where(causal, scores, negative_big)
        expos = jnp.exp(scores - jnp.max(scores, axis=-1, keepdims=True))
        sums = jnp.sum(expos, axis=-1, keepdims=True)
        weighted = (jnp.dot(expos.astype(jnp.bfloat16), values, preferred_element_type=f32) / sums).astype(jnp.bfloat16)
        for head in range(HEADS):
            out_ref[at, head * HD : (head + 1) * HD] = weighted[head * SEQ_LEN : (head + 1) * SEQ_LEN]


def prefill(place, mine, other):
    return pl.pallas_call(
        prefill_kernel,
        in_specs=smem(1) + vmem(2),
        out_specs=pl.BlockSpec(memory_space=pltpu.VMEM),
        out_shape=bf16(ROWS, WIDTH),
        compiler_params=params(),
        cost_estimate=pl.CostEstimate(flops=140_000_000, bytes_accessed=1_200_000, transcendentals=262144),
        name="prefill_attention",
    )(place, mine, other)


def partial_kernel(x_ref, qw_ref, kv_ref, out_ref):
    x = x_ref[...]
    for col, part in ((0, jnp.dot(x, qw_ref[...], preferred_element_type=f32)), (8, jnp.dot(x, kv_ref[...], preferred_element_type=f32))):
        for i in range(BATCH // 8):
            for j in range(part.shape[1] // HD):
                out_ref[i * 10 + col + j] = part[i * 8 : (i + 1) * 8, j * HD : (j + 1) * HD]
    out_ref[60:] = jnp.zeros((4, 8, HD), f32)


def partial(x, qw, kv):
    return pl.pallas_call(
        partial_kernel,
        in_specs=vmem(3),
        out_specs=pl.BlockSpec(memory_space=pltpu.VMEM),
        out_shape=shaped(f32, 64, 8, HD),
        compiler_params=params(),
        name="decode_partial",
    )(x, qw, kv)


def total_kernel(in_ref, out_ref):
    both = [jnp.sum(in_ref[:, m], axis=0) for m in range(2)]
    done = jnp.concatenate(both, axis=0).astype(jnp.bfloat16)
    out_ref[...] = jnp.broadcast_to(done[None], out_ref.shape)


def total(shares):
    return pl.pallas_call(
        total_kernel,
        in_specs=vmem(1),
        out_specs=pl.BlockSpec(memory_space=pltpu.VMEM),
        out_shape=bf16(COUNT, 16, HD),
        compiler_params=params(),
        name="decode_total",
    )(shares.reshape(COUNT, 2, 8, HD))


def decode_kernel(place_ref, length_ref, tile_ref, key_hbm, value_hbm, out_ref, rows_ref, score_ref, length_rows, key_ref, value_ref, sems):
    loads = [pltpu.make_async_copy(key_hbm, key_ref, sems.at[0]), pltpu.make_async_copy(value_hbm, value_ref, sems.at[1])]
    for load in loads:
        load.start()
    rep = place_ref[3]
    with_own = rep == 0
    for i in range(BATCH // 8):
        for j in range(10):
            t = i * 10 + j
            tile = tile_ref[t // 2, (t % 2) * 8 : (t % 2 + 1) * 8, :].astype(f32)
            rows_ref[i * 8 : (i + 1) * 8, j, :] = tile
    loads[0].wait()
    for b in range(BATCH):
        score_ref[b] = lax.dot_general(
            rows_ref[b, 0:8].astype(jnp.bfloat16), key_ref[b], (((1,), (1,)), ((), ())), preferred_element_type=f32
        )
        length_rows[b] = jnp.full((8, HD), length_ref[b], jnp.int32)
    lane = lax.broadcasted_iota(jnp.int32, (8, HD), 1)
    position = (rep * key_ref.shape[1] + lane)[None]
    loads[1].wait()
    for i in range(BATCH // 8):
        at = slice(i * 8, (i + 1) * 8)
        scores = score_ref[at] * SCALE
        own = jnp.sum(rows_ref[at, 0:8] * rows_ref[at, 8:9], axis=-1, keepdims=True) * SCALE
        allowed = position < length_rows[at]
        own = jnp.where(with_own, own, negative_big)
        top = jnp.maximum(jnp.max(jnp.where(allowed, scores, negative_big), axis=-1, keepdims=True), own)
        expos = jnp.where(allowed, jnp.exp(scores - top), 0.0)
        own_exp = jnp.where(with_own, jnp.exp(own - top), 0.0)
        sums = jnp.sum(expos, axis=-1, keepdims=True) + own_exp
        extra = own_exp.astype(jnp.bfloat16).astype(f32) * rows_ref[at, 9:10]
        weights = expos.astype(jnp.bfloat16)
        for k in range(0, 8, 2):
            pair = (i * 8 + k) // 2
            for m in range(2):
                outs = jnp.dot(weights[k + m], value_ref[i * 8 + k + m], preferred_element_type=f32)
                out_ref[pair, 8 * m : 8 * (m + 1)] = outs + extra[k + m]
            stats = jnp.where(lane == 0, top[k], jnp.where(lane == 1, sums[k], 1.0))
            out_ref[pair, 16:24] = jnp.where(lane == 2, top[k + 1], jnp.where(lane == 3, sums[k + 1], stats))
    out_ref[BATCH // 2 :] = jnp.ones((COUNT - BATCH // 2, 24, HD), f32)


def decode(place, lengths, tiles, keys, values):
    return pl.pallas_call(
        decode_kernel,
        in_specs=smem(2) + vmem(1) + anywhere(2),
        out_specs=pl.BlockSpec(memory_space=pltpu.VMEM),
        out_shape=shaped(f32, COUNT, 24, HD),
        scratch_shapes=[
            pltpu.VMEM((BATCH, 16, HD), f32),
            pltpu.VMEM((BATCH, 8, HD), f32),
            pltpu.VMEM((BATCH, 8, HD), jnp.int32),
            pltpu.VMEM((BATCH, HD, HD), jnp.bfloat16),
            pltpu.VMEM((BATCH, HD, HD), jnp.bfloat16),
            pltpu.SemaphoreType.DMA((2,)),
        ],
        compiler_params=params(),
        cost_estimate=pl.CostEstimate(flops=30_000_000, bytes_accessed=4_000_000, transcendentals=50000),
        name="decode_attention",
    )(place, lengths, tiles, keys, values)


def combine_kernel(in_ref, out_ref):
    stats = in_ref[:, 16:24]
    done = []
    for m in range(2):
        tops, sums = stats[:, :, 2 * m : 2 * m + 1], stats[:, :, 2 * m + 1 : 2 * m + 2]
        keep = jnp.exp(tops - jnp.max(tops, axis=0, keepdims=True))
        numer = jnp.sum(in_ref[:, 8 * m : 8 * (m + 1)] * keep, axis=0)
        done.append(numer / jnp.sum(sums * keep, axis=0))
    done = jnp.concatenate(done, axis=0).astype(jnp.bfloat16)
    out_ref[...] = jnp.broadcast_to(done[None], out_ref.shape)


def combine(parts):
    return pl.pallas_call(
        combine_kernel,
        in_specs=vmem(1),
        out_specs=pl.BlockSpec(memory_space=pltpu.VMEM),
        out_shape=bf16(COUNT, 16, HD),
        compiler_params=params(),
        name="decode_combine",
    )(parts)


def swap_all(value):
    return lax.all_to_all(value, REP, 0, 0, tiled=True)


def per_device(prefill_x, decode_x, query_weight, keyvalue_weight, key_cache, value_cache, cache_lengths, chain_order):
    xl, z, c = lax.axis_index("xl"), lax.axis_index("z"), lax.axis_index("c")
    xh, y = lax.axis_index("xh"), lax.axis_index("y")
    x = xh * 2 + xl
    rep = xl * 16 + z * 2 + c
    place = jnp.stack([xl, x, y, rep]).astype(jnp.int32)
    blocks = jnp.arange(COUNT, dtype=jnp.int32)

    barrier = lax.optimization_barrier
    block = jnp.sum(jnp.where(chain_order == rep, blocks, 0))
    piece_x = lax.dynamic_slice(decode_x, (0, (block % 4) * ROWS), (BATCH, ROWS))
    piece_x = jnp.where(block // 4 == xh * 4 + y, piece_x, jnp.zeros_like(piece_x))

    kept, given = split(place, query_weight, keyvalue_weight)
    got = ring(given, "xl", 2, 1)
    xb = around(prefill_x[128:], "y")
    piece_x = piece_x + ring(piece_x, "xh", 2, 1)
    got, piece_x, xb[1], xb[2] = barrier((got, piece_x, xb[1], xb[2]))
    weights = lax.all_gather(jnp.stack([kept, got]), ("z", "c"))

    piece_x = piece_x + ring(piece_x, "y", 4, 1) + ring(piece_x, "y", 4, -1) + ring(piece_x, "y", 4, 2)
    xa = around(prefill_x[:128], X)
    shares = partial(piece_x, query_weight, keyvalue_weight)
    shares, *xs = barrier((shares, *xa, *xb))
    shares = swap_all(shares)

    xa, xb = pack(xs[:4]), pack(xs[4:])
    xa, xb = around(xa, "y"), [xb, ring(xb, X, 4, 1), ring(xb, X, 4, -1)]
    shares, xb[1], xb[2] = barrier((shares, xb[1], xb[2]))
    tiles = total(shares)
    tiles, opposite = barrier((tiles, xb[0]))
    xb.append(ring(opposite, X, 4, 2))
    tiles = swap_all(tiles)
    parts = swap_all(decode(place, cache_lengths, tiles, key_cache, value_cache))

    near = jnp.arange(16, dtype=jnp.int32)
    stored = jnp.stack([xl * 16 + near, (1 - xl) * 16 + near], axis=1).reshape(COUNT)
    logical = jnp.sum(jnp.where(chain_order[None, :] == stored[:, None], blocks[None, :], 0), axis=1)
    theirs, mine = project(place, logical, xa, xb, weights.reshape(8, 4 * ROWS, HALF))
    theirs, parts = barrier((theirs, parts))
    other = ring(theirs, "xl", 2, 1)
    attn_dec = swap_all(combine(parts))[: BATCH // 2].reshape(BATCH, WIDTH)
    attn_pre = prefill(place, mine, other)
    return attn_pre, attn_dec


def solution(mesh):
    fine = Mesh(np.asarray(mesh.devices).reshape(2, 8, 2, 2, 4), ("xl", "z", "c", "xh", "y"))
    rep, tp = REP, ("xh", "y")
    in_specs = (P(rep, tp), P(None, tp), P(rep, tp), P(rep, tp), P(None, rep, tp), P(None, rep, tp), P(), P())
    out_specs = (P(rep, tp), P(None, tp))
    return jax.shard_map(per_device, mesh=fine, in_specs=in_specs, out_specs=out_specs, check_vma=False)
```

time: 167 us -> 158 us (0.946)
  local copies, waits for them, and re-layouts: 30.2 us -> 8.5 us
  waiting for transfers between devices: 55.6 us -> 34.2 us
  blocking collectives: 0 us -> 16.3 us
  starting transfers between devices: 41.5 us -> 52.8 us
  Pallas kernels: 19.3 us -> 27.3 us
  matrix products: 3.16 us -> 0 us
  between operations: 14.4 us -> 16.9 us
    all_to_all x2 -> x3, starting transfers between devices: 11.8 us -> 30.1 us  [swap_all(): return lax.all_to_all(value, REP, 0, 0, tiled=True)]
    ppermute x19 -> x18, waiting for transfers between devices: 28.3 us -> 10 us  [ring(): return lax.ppermute(value, axes, pairs)]
    all_to_all x0 -> x1, blocking collectives: none -> 16.3 us  [swap_all(): return lax.all_to_all(value, REP, 0, 0, tiled=True)]
    all_gather x2 -> x1, waiting for transfers between devices: 14.9 us -> 0.02 us  [per_device(): weights = lax.all_gather(jnp.stack([kept, got]), ('z', 'c'))]
    unnamed x31 -> x34, local copies, waits for them, and re-layouts: 20.1 us -> 6.51 us
    all_to_all x2 -> x3, waiting for transfers between devices: 12.4 us -> 24.1 us  [swap_all(): return lax.all_to_all(value, REP, 0, 0, tiled=True)]
    pallas_call x2 -> x9, Pallas kernels: 19.3 us -> 27.3 us  [the longest x1 17.2 us: project(): pl.pallas_call(project_kernel, in_specs=smem(2) + anywhere(9), out_specs=...]
    ppermute x19 -> x18, starting transfers between devices: 28.4 us -> 22.6 us  [ring(): return lax.ppermute(value, axes, pairs)]
  transfers between devices with their start and end apart: 24 -> 22, of which waited for: 9 -> 5; matrix products, arithmetic and copies ran while one was open for 14% -> 1% of each run, Pallas kernels for 3% -> 16%
where the time goes in v2:
time: 158 us
  starting transfers between devices  52.8 us (33%)
  waiting for transfers between devices  34.2 us (22%)
  Pallas kernels  27.3 us (17%)
  between operations  16.9 us (11%)
  blocking collectives  16.3 us (10%)
  local copies, waits for them, and re-layouts  8.5 us (5%)
  other arithmetic  1.89 us (1%)
    all_to_all x3, starting transfers between devices, swap_all(): return lax.all_to_all(value, REP, 0, 0, tiled=True)  30.1 us
    all_to_all x3, waiting for transfers between devices, swap_all(): return lax.all_to_all(value, REP, 0, 0, tiled=True)  24.1 us
    ppermute x18, starting transfers between devices, ring(): return lax.ppermute(value, axes, pairs)  22.6 us
    pallas_call x1, Pallas kernels, project(): pl.pallas_call(project_kernel, in_specs=smem(2) + anywhere(9), out_specs=...  17.2 us
    all_to_all x1, blocking collectives, swap_all(): return lax.all_to_all(value, REP, 0, 0, tiled=True)  16.3 us
    ppermute x18, waiting for transfers between devices, ring(): return lax.ppermute(value, axes, pairs)  10 us
    unnamed x34, local copies, waits for them, and re-layouts  6.51 us
    pallas_call x1, Pallas kernels, decode(): pl.pallas_call(decode_kernel, in_specs=smem(2) + vmem(1) + anywhere(2), o...  3.19 us
  transfers between devices with their start and end apart: 22, of which 5 were waited for; matrix products, arithmetic and copies ran while one was open for 1% of the time, Pallas kernels for 16%

profile of v2, /device:TPU:1, one launch (start us, length us, event | category | flops | bytes accessed | tf_op | source)
XLA Modules:
  0.0 157.9 jit_solution(12059528355425681176)
XLA Ops:
  7.3 1.1 fusion.1
  8.4 2.2 %collective-permute-start.2 = (bf16[128,1024]{1,0:T(8,128)(2,1)S(1)}, bf16[128,1024]{1,0:T(8,128)(2,1)S(1)}, u32[]{:S(2)}, u32[]{:S(2)}) collective-permute-start(bf16[128,1024]{1,0:T(8,128)(2,1)S(1)} %get-tuple-element.34.refs_0_), channel_id=1, source_target_pairs={{0,1},{1,2},{2,3},{3,0},{4,5},{5,6},{6,7},{7,4},{8,9},{9,10},{10,1... | collective-permute-start | bytes 786440 | tf_op jit(solution)/shard_map/ppermute | solution.py:38
  10.6 1.5 collective-permute-start.3
  12.1 0.1 pad_add_fusion.1.place_ref
  12.2 1.0 copy-done
  13.3 0.9 copy-done.6
  14.2 0.7 split.1
  14.8 1.3 collective-permute-start
  16.1 0.7 fusion
  19.4 2.5 %collective-permute-start.1 = (bf16[48,256]{1,0:T(8,128)(2,1)S(1)}, bf16[48,256]{1,0:T(8,128)(2,1)S(1)}, u32[]{:S(2)}, u32[]{:S(2)}) collective-permute-start(bf16[48,256]{1,0:T(8,128)(2,1)S(1)} %dynamic-slice_select_fusion), channel_id=1, source_target_pairs={{0,4},{4,0},{1,5},{5,1},{2,6},{6,2},{3,7},{7,3},{8,12},{12,8},{9,1... | collective-permute-start | bytes 73736 | tf_op jit(solution)/shard_map/ppermute | solution.py:38
  21.9 3.5 %collective-permute-done.1 = bf16[48,256]{1,0:T(8,128)(2,1)S(1)} collective-permute-done((bf16[48,256]{1,0:T(8,128)(2,1)S(1)}, bf16[48,256]{1,0:T(8,128)(2,1)S(1)}, u32[]{:S(2)}, u32[]{:S(2)}) %collective-permute-start.1) | collective-permute-done | bytes 24608 | tf_op jit(solution)/shard_map/ppermute | solution.py:38
  25.5 0.9 pad_maximum_fusion
  26.4 1.5 collective-permute-start.6
  27.9 0.8 collective-permute-start.5
  28.7 2.7 %collective-permute-start.8 = (bf16[128,1024]{1,0:T(8,128)(2,1)S(1)}, bf16[128,1024]{1,0:T(8,128)(2,1)S(1)}, u32[]{:S(2)}, u32[]{:S(2)}) collective-permute-start(bf16[128,1024]{1,0:T(8,128)(2,1)S(1)} %get-tuple-element.30.refs_0_), channel_id=1, source_target_pairs={{0,132},{128,0},{4,128},{132,4},{1,133},{129,1},{5,129},{133,5},{2... | collective-permute-start | bytes 786440 | tf_op jit(solution)/shard_map/ppermute | solution.py:38
  31.4 1.4 collective-permute-start.10
  32.8 0.2 collective-permute-start.4
  33.0 5.6 %collective-permute-done.4 = bf16[48,256]{1,0:T(8,128)(2,1)S(1)} collective-permute-done((bf16[48,256]{1,0:T(8,128)(2,1)S(1)}, bf16[48,256]{1,0:T(8,128)(2,1)S(1)}, u32[]{:S(2)}, u32[]{:S(2)}) %collective-permute-start.4) | collective-permute-done | bytes 24608 | tf_op jit(solution)/shard_map/ppermute | solution.py:38
  38.7 0.9 decode_partial.1
  39.7 0.7 copy-done.8
  40.4 0.8 collective-permute-done.9.refs_3_
  41.2 1.1 pack.3.refs_4_
  42.3 2.7 %collective-permute-start.15 = (bf16[512,1024]{1,0:T(8,128)(2,1)}, bf16[512,1024]{1,0:T(8,128)(2,1)}, u32[]{:S(2)}, u32[]{:S(2)}) collective-permute-start(bf16[512,1024]{1,0:T(8,128)(2,1)} %pack.3.refs_4_), channel_id=1, source_target_pairs={{0,132},{128,0},{4,128},{132,4},{1,133},{129,1},{5,129},{133,5},{2... | collective-permute-start | bytes 3145736 | tf_op jit(solution)/shard_map/ppermute | solution.py:38
  44.9 13.4 %all-to-all-start = ((f32[64,8,128]{2,1,0:T(8,128)}), f32[64,8,128]{2,1,0:T(8,128)S(1)}, u32[]{:S(2)}, u32[]{:S(2)}) async-start(f32[64,8,128]{2,1,0:T(8,128)} %decode_partial.1), calls=%async_computation | async-start | bytes 524288 | tf_op jit(solution)/shard_map/all_to_all | solution.py:335
  58.4 0.9 copy-done.5
  59.3 1.0 copy-done.9
  60.3 0.9 copy-done.11
  61.2 1.0 copy-done.13
  62.2 1.1 pack.2.refs_0_
  63.3 0.7 collective-permute-start.11
  63.9 2.0 %collective-permute-start.12 = (bf16[512,1024]{1,0:T(8,128)(2,1)}, bf16[512,1024]{1,0:T(8,128)(2,1)}, u32[]{:S(2)}, u32[]{:S(2)}) collective-permute-start(bf16[512,1024]{1,0:T(8,128)(2,1)} %pack.2.refs_0_), channel_id=1, source_target_pairs={{0,3},{1,0},{2,1},{3,2},{4,7},{5,4},{6,5},{7,6},{8,11},{9,8},{10,9... | collective-permute-start | bytes 3145736 | tf_op jit(solution)/shard_map/ppermute | solution.py:38
  65.9 0.2 collective-permute-start.13
  66.1 6.9 %all-to-all-done = f32[64,8,128]{2,1,0:T(8,128)S(1)} async-done(((f32[64,8,128]{2,1,0:T(8,128)}), f32[64,8,128]{2,1,0:T(8,128)S(1)}, u32[]{:S(2)}, u32[]{:S(2)}) %all-to-all-start) | async-done | bytes 262176 | tf_op jit(solution)/shard_map/all_to_all | solution.py:335
  73.0 0.7 decode_total.1
  73.7 1.5 collective-permute-start.16
  75.2 7.7 %all-to-all-start.1 = ((bf16[32,16,128]{2,1,0:T(8,128)(2,1)}), bf16[32,16,128]{2,1,0:T(8,128)(2,1)S(1)}, u32[]{:S(2)}, u32[]{:S(2)}) async-start(bf16[32,16,128]{2,1,0:T(8,128)(2,1)} %decode_total.1), calls=%async_computation.1 | async-start | bytes 262144 | tf_op jit(solution)/shard_map/all_to_all | solution.py:335
  82.9 17.3 %all-to-all-done.1.tile_ref = bf16[32,16,128]{2,1,0:T(8,128)(2,1)S(1)} async-done(((bf16[32,16,128]{2,1,0:T(8,128)(2,1)}), bf16[32,16,128]{2,1,0:T(8,128)(2,1)S(1)}, u32[]{:S(2)}, u32[]{:S(2)}) %all-to-all-start.1) | async-done | bytes 131104 | tf_op jit(solution)/shard_map/all_to_all | solution.py:335
  100.2 3.2 %decode_attention.1 = f32[32,24,128]{2,1,0:T(8,128)} custom-call(s32[4]{0:T(128)S(1)} %pad_add_fusion.1.place_ref, s32[48]{0:T(128)S(1)} %copy-done.14, bf16[32,16,128]{2,1,0:T(8,128)(2,1)S(1)} %all-to-all-done.1.tile_ref, bf16[48,128,128]{2,1,0:T(8,128)(2,1)S(1)} %copy-done.2, bf16[48,128,128]{2,1,0:T(8,128)(2,1)S(1)} %copy-done.3), custom_call_target="tpu_custom_call" | custom-call | flops 30000000 | bytes 4000000 | tf_op jit(solution)/shard_map/decode_attention/pallas_call | solution.py:292
  103.4 8.9 %all-to-all-start.2 = ((f32[32,24,128]{2,1,0:T(8,128)}), f32[32,24,128]{2,1,0:T(8,128)S(1)}, u32[]{:S(2)}, u32[]{:S(2)}) async-start(f32[32,24,128]{2,1,0:T(8,128)} %decode_attention.1), calls=%async_computation.2 | async-start | bytes 786432 | tf_op jit(solution)/shard_map/all_to_all | solution.py:335
  112.4 0.1 copy.11
  112.5 0.1 eq.27
  112.6 0.2 select_reduce_fusion.logical_ref
  112.8 17.2 %project.1 = (bf16[256,640]{1,0:T(8,128)(2,1)S(1)}, bf16[256,640]{1,0:T(8,128)(2,1)S(1)}) custom-call(s32[4]{0:T(128)S(1)} %pad_add_fusion.1.place_ref, s32[32]{0:T(128)S(1)} %select_reduce_fusion.logical_ref, bf16[512,1024]{1,0:T(8,128)(2,1)} %pack.2.refs_0_, bf16[512,1024]{1,0:T(8,128)(2,1)} %collective-permute-done.11.refs_1_, ...), custom_call_target="tpu_custom_call" | custom-call | flops 5368709120 | bytes 19000000 | tf_op jit(solution)/shard_map/project/pallas_call | solution.py:158
  130.0 1.5 collective-permute-start.17
  131.5 0.3 decode_combine.1
  131.8 16.3 %all_to_all.20 = bf16[32,16,128]{2,1,0:T(8,128)(2,1)S(1)} all-to-all(bf16[32,16,128]{2,1,0:T(8,128)(2,1)S(1)} %decode_combine.1), channel_id=1, replica_groups=mesh['xl'=2,'z'=8,'c'=2,'xh'=2,'y'=4] {'xl','z','c'}, dimensions={0} | all-to-all | bytes 262144 | tf_op jit(solution)/shard_map/all_to_all | solution.py:335
  148.1 0.7 reshape.31
  148.8 2.2 %prefill_attention.1 = bf16[256,1024]{1,0:T(8,128)(2,1)} custom-call(s32[4]{0:T(128)S(1)} %pad_add_fusion.1.place_ref, bf16[256,640]{1,0:T(8,128)(2,1)S(1)} %get-tuple-element.45.mine_ref, bf16[256,640]{1,0:T(8,128)(2,1)S(1)} %collective-permute-done.17.other_ref), custom_call_target="tpu_custom_call" | custom-call | flops 140000000 | bytes 1200000 | tf_op jit(solution)/shard_map/prefill_attention/pallas_call | solution.py:201
  (56 shorter events, 0.2 us)
Async XLA Ops:
  7.2 9.0 %copy-start.16 = (s32[32]{0:T(128)S(1)}, s32[32]{0:T(128)}, u32[]{:S(2)}) copy-start(s32[32]{0:T(128)} %param.15) | copy-start | bytes 388
  7.2 12.2 %copy-start.15 = (bf16[48,1024]{1,0:T(8,128)(2,1)S(1)}, bf16[48,1024]{1,0:T(8,128)(2,1)}, u32[]{:S(2)}) copy-start(bf16[48,1024]{1,0:T(8,128)(2,1)} %param.9) | copy-start | bytes 294916
  7.2 105.6 %all-gather.3.cloned.1.call-start = ((), (), s32[]{:S(2)}) async-start(), calls=%async_computation.4 | async-start | bytes 11141120 | tf_op jit(solution)/shard_map/all_gather | solution.py:356
  7.2 31.5 %copy-start.1 = (bf16[256,1024]{1,0:T(8,128)(2,1)S(1)}, bf16[256,1024]{1,0:T(8,128)(2,1)}, u32[]{:S(2)}) copy-start(bf16[256,1024]{1,0:T(8,128)(2,1)} %qw_ref.3) | copy-start | bytes 1572868
  7.2 31.5 %copy-start.7 = (bf16[256,256]{1,0:T(8,128)(2,1)S(1)}, bf16[256,256]{1,0:T(8,128)(2,1)}, u32[]{:S(2)}) copy-start(bf16[256,256]{1,0:T(8,128)(2,1)} %kv_ref.3) | copy-start | bytes 393220
  8.4 31.3 %copy-start.4 = (bf16[128,1024]{1,0:T(8,128)(2,1)}, bf16[128,1024]{1,0:T(8,128)(2,1)S(1)}, u32[]{:S(2)}) copy-start(bf16[128,1024]{1,0:T(8,128)(2,1)S(1)} %get-tuple-element.30.refs_0_) | copy-start | bytes 786436
  8.4 17.1 %collective-permute-start.2 = (bf16[128,1024]{1,0:T(8,128)(2,1)S(1)}, bf16[128,1024]{1,0:T(8,128)(2,1)S(1)}, u32[]{:S(2)}, u32[]{:S(2)}) collective-permute-start(bf16[128,1024]{1,0:T(8,128)(2,1)S(1)} %get-tuple-element.34.refs_0_), channel_id=1, source_target_pairs={{0,1},{1,2},{2,3},{3,0},{4,5},{5,6},{6,7},{7,4},{8,9},{9,10},{10,1... | collective-permute-start | bytes 786440 | tf_op jit(solution)/shard_map/ppermute | solution.py:38
  10.6 14.9 %collective-permute-start.3 = (bf16[128,1024]{1,0:T(8,128)(2,1)S(1)}, bf16[128,1024]{1,0:T(8,128)(2,1)S(1)}, u32[]{:S(2)}, u32[]{:S(2)}) collective-permute-start(bf16[128,1024]{1,0:T(8,128)(2,1)S(1)} %get-tuple-element.34.refs_0_), channel_id=1, source_target_pairs={{0,3},{1,0},{2,1},{3,2},{4,7},{5,4},{6,5},{7,6},{8,11},{9,8},{10,9... | collective-permute-start | bytes 786440 | tf_op jit(solution)/shard_map/ppermute | solution.py:38
  12.2 1.0 copy-start
  13.2 0.9 copy-start.6
  14.8 10.7 %collective-permute-start = (bf16[256,640]{1,0:T(8,128)(2,1)S(1)}, bf16[256,640]{1,0:T(8,128)(2,1)S(1)}, u32[]{:S(2)}, u32[]{:S(2)}) collective-permute-start(bf16[256,640]{1,0:T(8,128)(2,1)S(1)} %get-tuple-element.26), channel_id=1, source_target_pairs={{0,128},{128,0},{1,129},{129,1},{2,130},{130,2},{3,131},{131,3},{4... | collective-permute-start | bytes 983048 | tf_op jit(solution)/shard_map/ppermute | solution.py:38
  19.4 6.1 %collective-permute-start.1 = (bf16[48,256]{1,0:T(8,128)(2,1)S(1)}, bf16[48,256]{1,0:T(8,128)(2,1)S(1)}, u32[]{:S(2)}, u32[]{:S(2)}) collective-permute-start(bf16[48,256]{1,0:T(8,128)(2,1)S(1)} %dynamic-slice_select_fusion), channel_id=1, source_target_pairs={{0,4},{4,0},{1,5},{5,1},{2,6},{6,2},{3,7},{7,3},{8,12},{12,8},{9,1... | collective-permute-start | bytes 73736 | tf_op jit(solution)/shard_map/ppermute | solution.py:38
  26.4 4.9 %collective-permute-start.6 = (bf16[48,256]{1,0:T(8,128)(2,1)S(1)}, bf16[48,256]{1,0:T(8,128)(2,1)S(1)}, u32[]{:S(2)}, u32[]{:S(2)}) collective-permute-start(bf16[48,256]{1,0:T(8,128)(2,1)S(1)} %fusion.2), channel_id=1, source_target_pairs={{0,2},{1,3},{2,0},{3,1},{4,6},{5,7},{6,4},{7,5},{8,10},{9,11},{10,... | collective-permute-start | bytes 73736 | tf_op jit(solution)/shard_map/ppermute | solution.py:38
  27.9 4.9 %collective-permute-start.5 = (bf16[48,256]{1,0:T(8,128)(2,1)S(1)}, bf16[48,256]{1,0:T(8,128)(2,1)S(1)}, u32[]{:S(2)}, u32[]{:S(2)}) collective-permute-start(bf16[48,256]{1,0:T(8,128)(2,1)S(1)} %fusion.2), channel_id=1, source_target_pairs={{0,3},{1,0},{2,1},{3,2},{4,7},{5,4},{6,5},{7,6},{8,11},{9,8},{10,9... | collective-permute-start | bytes 73736 | tf_op jit(solution)/shard_map/ppermute | solution.py:38
  28.7 10.9 %collective-permute-start.7 = (bf16[128,1024]{1,0:T(8,128)(2,1)S(1)}, bf16[128,1024]{1,0:T(8,128)(2,1)S(1)}, u32[]{:S(2)}, u32[]{:S(2)}) collective-permute-start(bf16[128,1024]{1,0:T(8,128)(2,1)S(1)} %get-tuple-element.30.refs_0_), channel_id=1, source_target_pairs={{0,128},{128,4},{4,132},{132,0},{1,129},{129,5},{5,133},{133,1},{2... | collective-permute-start | bytes 786440 | tf_op jit(solution)/shard_map/ppermute | solution.py:38
  28.7 11.6 %collective-permute-start.8 = (bf16[128,1024]{1,0:T(8,128)(2,1)S(1)}, bf16[128,1024]{1,0:T(8,128)(2,1)S(1)}, u32[]{:S(2)}, u32[]{:S(2)}) collective-permute-start(bf16[128,1024]{1,0:T(8,128)(2,1)S(1)} %get-tuple-element.30.refs_0_), channel_id=1, source_target_pairs={{0,132},{128,0},{4,128},{132,4},{1,133},{129,1},{5,129},{133,5},{2... | collective-permute-start | bytes 786440 | tf_op jit(solution)/shard_map/ppermute | solution.py:38
  31.4 9.8 %collective-permute-start.9 = (bf16[128,1024]{1,0:T(8,128)(2,1)S(1)}, bf16[128,1024]{1,0:T(8,128)(2,1)S(1)}, u32[]{:S(2)}, u32[]{:S(2)}) collective-permute-start(bf16[128,1024]{1,0:T(8,128)(2,1)S(1)} %get-tuple-element.30.refs_0_), channel_id=1, source_target_pairs={{0,4},{128,132},{4,0},{132,128},{1,5},{129,133},{5,1},{133,129},{2... | collective-permute-start | bytes 786440 | tf_op jit(solution)/shard_map/ppermute | solution.py:38
  31.4 9.8 %collective-permute-start.10 = (bf16[128,1024]{1,0:T(8,128)(2,1)S(1)}, bf16[128,1024]{1,0:T(8,128)(2,1)S(1)}, u32[]{:S(2)}, u32[]{:S(2)}) collective-permute-start(bf16[128,1024]{1,0:T(8,128)(2,1)S(1)} %get-tuple-element.34.refs_0_), channel_id=1, source_target_pairs={{0,2},{1,3},{2,0},{3,1},{4,6},{5,7},{6,4},{7,5},{8,10},{9,11},{10,... | collective-permute-start | bytes 786440 | tf_op jit(solution)/shard_map/ppermute | solution.py:38
  32.8 5.9 %collective-permute-start.4 = (bf16[48,256]{1,0:T(8,128)(2,1)S(1)}, bf16[48,256]{1,0:T(8,128)(2,1)S(1)}, u32[]{:S(2)}, u32[]{:S(2)}) collective-permute-start(bf16[48,256]{1,0:T(8,128)(2,1)S(1)} %fusion.2), channel_id=1, source_target_pairs={{0,1},{1,2},{2,3},{3,0},{4,5},{5,6},{6,7},{7,4},{8,9},{9,10},{10,1... | collective-permute-start | bytes 73736 | tf_op jit(solution)/shard_map/ppermute | solution.py:38
  39.6 0.7 copy-start.8
  40.3 1.9 %copy-start.10 = (bf16[128,1024]{1,0:T(8,128)(2,1)}, bf16[128,1024]{1,0:T(8,128)(2,1)S(1)}, u32[]{:S(2)}) copy-start(bf16[128,1024]{1,0:T(8,128)(2,1)S(1)} %collective-permute-done.8.refs_2_) | copy-start | bytes 786436
  41.2 1.1 copy-start.12
  41.2 59.0 %copy-start.14 = (s32[48]{0:T(128)S(1)}, s32[48]{0:T(128)}, u32[]{:S(2)}) copy-start(s32[48]{0:T(128)} %length_ref.1) | copy-start | bytes 580
  42.3 58.0 %copy-start.2 = (bf16[48,128,128]{2,1,0:T(8,128)(2,1)S(1)}, bf16[48,128,128]{2,1,0:T(8,128)(2,1)}, u32[]{:S(2)}) copy-start(bf16[48,128,128]{2,1,0:T(8,128)(2,1)} %key_hbm.1) | copy-start | bytes 4718596
  42.3 58.0 %copy-start.3 = (bf16[48,128,128]{2,1,0:T(8,128)(2,1)S(1)}, bf16[48,128,128]{2,1,0:T(8,128)(2,1)}, u32[]{:S(2)}) copy-start(bf16[48,128,128]{2,1,0:T(8,128)(2,1)} %value_hbm.1) | copy-start | bytes 4718596
  42.3 30.7 %collective-permute-start.14 = (bf16[512,1024]{1,0:T(8,128)(2,1)}, bf16[512,1024]{1,0:T(8,128)(2,1)}, u32[]{:S(2)}, u32[]{:S(2)}) collective-permute-start(bf16[512,1024]{1,0:T(8,128)(2,1)} %pack.3.refs_4_), channel_id=1, source_target_pairs={{0,128},{128,4},{4,132},{132,0},{1,129},{129,5},{5,133},{133,1},{2... | collective-permute-start | bytes 3145736 | tf_op jit(solution)/shard_map/ppermute | solution.py:38
  42.3 30.7 %collective-permute-start.15 = (bf16[512,1024]{1,0:T(8,128)(2,1)}, bf16[512,1024]{1,0:T(8,128)(2,1)}, u32[]{:S(2)}, u32[]{:S(2)}) collective-permute-start(bf16[512,1024]{1,0:T(8,128)(2,1)} %pack.3.refs_4_), channel_id=1, source_target_pairs={{0,132},{128,0},{4,128},{132,4},{1,133},{129,1},{5,129},{133,5},{2... | collective-permute-start | bytes 3145736 | tf_op jit(solution)/shard_map/ppermute | solution.py:38
  44.9 28.0 %all-to-all-start = ((f32[64,8,128]{2,1,0:T(8,128)}), f32[64,8,128]{2,1,0:T(8,128)S(1)}, u32[]{:S(2)}, u32[]{:S(2)}) async-start(f32[64,8,128]{2,1,0:T(8,128)} %decode_partial.1), calls=%async_computation | async-start | bytes 524288 | tf_op jit(solution)/shard_map/all_to_all | solution.py:335
  58.4 1.0 copy-start.5
  59.3 1.0 copy-start.9
  60.3 0.9 copy-start.11
  61.2 1.0 copy-start.13
  63.3 49.5 %collective-permute-start.11 = (bf16[512,1024]{1,0:T(8,128)(2,1)}, bf16[512,1024]{1,0:T(8,128)(2,1)}, u32[]{:S(2)}, u32[]{:S(2)}) collective-permute-start(bf16[512,1024]{1,0:T(8,128)(2,1)} %pack.2.refs_0_), channel_id=1, source_target_pairs={{0,1},{1,2},{2,3},{3,0},{4,5},{5,6},{6,7},{7,4},{8,9},{9,10},{10,1... | collective-permute-start | bytes 3145736 | tf_op jit(solution)/shard_map/ppermute | solution.py:38
  63.9 48.8 %collective-permute-start.12 = (bf16[512,1024]{1,0:T(8,128)(2,1)}, bf16[512,1024]{1,0:T(8,128)(2,1)}, u32[]{:S(2)}, u32[]{:S(2)}) collective-permute-start(bf16[512,1024]{1,0:T(8,128)(2,1)} %pack.2.refs_0_), channel_id=1, source_target_pairs={{0,3},{1,0},{2,1},{3,2},{4,7},{5,4},{6,5},{7,6},{8,11},{9,8},{10,9... | collective-permute-start | bytes 3145736 | tf_op jit(solution)/shard_map/ppermute | solution.py:38
  65.9 46.9 %collective-permute-start.13 = (bf16[512,1024]{1,0:T(8,128)(2,1)}, bf16[512,1024]{1,0:T(8,128)(2,1)}, u32[]{:S(2)}, u32[]{:S(2)}) collective-permute-start(bf16[512,1024]{1,0:T(8,128)(2,1)} %pack.2.refs_0_), channel_id=1, source_target_pairs={{0,2},{1,3},{2,0},{3,1},{4,6},{5,7},{6,4},{7,5},{8,10},{9,11},{10,... | collective-permute-start | bytes 3145736 | tf_op jit(solution)/shard_map/ppermute | solution.py:38
  73.7 39.1 %collective-permute-start.16 = (bf16[512,1024]{1,0:T(8,128)(2,1)}, bf16[512,1024]{1,0:T(8,128)(2,1)}, u32[]{:S(2)}, u32[]{:S(2)}) collective-permute-start(bf16[512,1024]{1,0:T(8,128)(2,1)} %pack.3.refs_4_), channel_id=1, source_target_pairs={{0,4},{128,132},{4,0},{132,128},{1,5},{129,133},{5,1},{133,129},{2... | collective-permute-start | bytes 3145736 | tf_op jit(solution)/shard_map/ppermute | solution.py:38
  75.2 25.0 %all-to-all-start.1 = ((bf16[32,16,128]{2,1,0:T(8,128)(2,1)}), bf16[32,16,128]{2,1,0:T(8,128)(2,1)S(1)}, u32[]{:S(2)}, u32[]{:S(2)}) async-start(bf16[32,16,128]{2,1,0:T(8,128)(2,1)} %decode_total.1), calls=%async_computation.1 | async-start | bytes 262144 | tf_op jit(solution)/shard_map/all_to_all | solution.py:335
  103.4 26.6 %all-to-all-start.2 = ((f32[32,24,128]{2,1,0:T(8,128)}), f32[32,24,128]{2,1,0:T(8,128)S(1)}, u32[]{:S(2)}, u32[]{:S(2)}) async-start(f32[32,24,128]{2,1,0:T(8,128)} %decode_attention.1), calls=%async_computation.2 | async-start | bytes 786432 | tf_op jit(solution)/shard_map/all_to_all | solution.py:335
  130.0 18.8 %collective-permute-start.17 = (bf16[256,640]{1,0:T(8,128)(2,1)S(1)}, bf16[256,640]{1,0:T(8,128)(2,1)S(1)}, u32[]{:S(2)}, u32[]{:S(2)}) collective-permute-start(bf16[256,640]{1,0:T(8,128)(2,1)S(1)} %get-tuple-element.48), channel_id=1, source_target_pairs={{0,128},{128,0},{1,129},{129,1},{2,130},{130,2},{3,131},{131,3},{4... | collective-permute-start | bytes 983048 | tf_op jit(solution)/shard_map/ppermute | solution.py:38
Sparse Core Ops, SparseCore 0:
  26.6 76.1 all-gather.2

commit v3 on v2

--- a/solution.py
+++ b/solution.py
@@ -117,24 +117,23 @@
     )(*parts)
 
 
-def project_kernel(place_ref, logical_ref, *refs):
-    a_refs, b_refs, w_ref, theirs_ref, mine_ref = refs[:4], refs[4:8], refs[8], refs[9], refs[10]
-    x_all, w_all, acc, x_sem, w_sem = refs[11:]
+def project_kernel(slots, place_ref, logical_ref, *refs):
+    a_refs, b_refs, w_ref, out_ref = refs[:4], refs[4:8], refs[8], refs[9]
+    x_all, w_all, acc, x_sem, w_sem = refs[10:]
     x, y = place_ref[1], place_ref[2]
-    moves = []
-    for i in range(4):
-        for k in range(4):
-            base = ROWS if k in OWN else 0
-            group = (((x + STEPS[k]) % 4) // 2) * 4 + (y + STEPS[i]) % 4
-            moves.append((a_refs[i].at[k * 128 : (k + 1) * 128], x_all.at[group, base : base + 128]))
-            base = (ROWS if i in OWN else 0) + 128
-            group = (((x + STEPS[i]) % 4) // 2) * 4 + (y + STEPS[k]) % 4
-            moves.append((b_refs[i].at[k * 128 : (k + 1) * 128], x_all.at[group, base : base + 128]))
-    moves = [pltpu.make_async_copy(src, dst, x_sem.at[n]) for n, (src, dst) in enumerate(moves)]
+    copies = []
+    for n, slot in enumerate(slots):
+        at_x = (x + STEPS[slot]) % 4
+        for i in range(4):
+            at_y = (y + STEPS[i]) % 4
+            group = (at_x // 2) * 4 + at_y
+            copies.append((a_refs[i].at[slot * 128 : (slot + 1) * 128], x_all.at[group, :128], 2 * (4 * n + i)))
+            copies.append((b_refs[slot].at[i * 128 : (i + 1) * 128], x_all.at[group, 128:], 2 * (4 * n + i) + 1))
+    copies = [pltpu.make_async_copy(src, dst, x_sem.at[s]) for src, dst, s in copies]
     loads = [pltpu.make_async_copy(w_ref.at[i], w_all.at[i], w_sem.at[i]) for i in range(8)]
-    for copy in moves + loads:
+    for copy in copies + loads:
         copy.start()
-    for copy in moves:
+    for copy in copies:
         copy.wait()
     for i in range(8):
         loads[i].wait()
@@ -148,27 +147,24 @@
         elif i < 7:
             acc[...] += part
         else:
-            done = (acc[...] + part).astype(jnp.bfloat16)
-            theirs_ref[...] = done[:ROWS]
-            mine_ref[...] = done[ROWS:]
-
-
-def project(place, logical, a, b, w):
-    rows = 2 * ROWS
-    return pl.pallas_call(
-        project_kernel,
+            out_ref[...] = (acc[...] + part).astype(out_ref.dtype)
+
+
+def project(slots, place, logical, a, b, w):
+    return pl.pallas_call(
+        functools.partial(project_kernel, slots),
         in_specs=smem(2) + anywhere(9),
-        out_specs=vmem(2),
-        out_shape=[bf16(ROWS, HALF)] * 2,
+        out_specs=pl.BlockSpec(memory_space=pltpu.VMEM),
+        out_shape=bf16(ROWS, HALF),
         scratch_shapes=[
-            pltpu.VMEM((8, rows, WIDTH), jnp.bfloat16),
+            pltpu.VMEM((8, ROWS, WIDTH), jnp.bfloat16),
             pltpu.VMEM((8, 4 * ROWS, HALF), jnp.bfloat16),
-            pltpu.VMEM((rows, HALF), f32),
-            pltpu.SemaphoreType.DMA((32,)),
+            pltpu.VMEM((ROWS, HALF), f32),
+            pltpu.SemaphoreType.DMA((16,)),
             pltpu.SemaphoreType.DMA((8,)),
         ],
         compiler_params=params(48),
-        cost_estimate=pl.CostEstimate(flops=2 * rows * 8192 * HALF, bytes_accessed=19_000_000, transcendentals=0),
+        cost_estimate=pl.CostEstimate(flops=2 * ROWS * 8192 * HALF, bytes_accessed=15_000_000, transcendentals=0),
         name="project",
     )(place, logical, *a, *b, w)
 
@@ -302,7 +298,7 @@
             pltpu.VMEM((BATCH, HD, HD), jnp.bfloat16),
             pltpu.SemaphoreType.DMA((2,)),
         ],
-        compiler_params=params(),
+        compiler_params=params(56),
         cost_estimate=pl.CostEstimate(flops=30_000_000, bytes_accessed=4_000_000, transcendentals=50000),
         name="decode_attention",
     )(place, lengths, tiles, keys, values)
@@ -373,11 +369,14 @@
     near = jnp.arange(16, dtype=jnp.int32)
     stored = jnp.stack([xl * 16 + near, (1 - xl) * 16 + near], axis=1).reshape(COUNT)
     logical = jnp.sum(jnp.where(chain_order[None, :] == stored[:, None], blocks[None, :], 0), axis=1)
-    theirs, mine = project(place, logical, xa, xb, weights.reshape(8, 4 * ROWS, HALF))
+    weights = weights.reshape(8, 4 * ROWS, HALF)
+    theirs = project(PARTNER, place, logical, xa, xb, weights)
     theirs, parts = barrier((theirs, parts))
     other = ring(theirs, "xl", 2, 1)
-    attn_dec = swap_all(combine(parts))[: BATCH // 2].reshape(BATCH, WIDTH)
+    done = combine(parts)
+    mine = project(OWN, place, logical, xa, xb, weights)
     attn_pre = prefill(place, mine, other)
+    attn_dec = swap_all(done)[: BATCH // 2].reshape(BATCH, WIDTH)
     return attn_pre, attn_dec
 
 

time: 158 us -> 155 us (0.981)
  waiting for transfers between devices: 34.2 us -> 24.7 us
  blocking collectives: 16.3 us -> 24.8 us
  starting transfers between devices: 52.8 us -> 50.3 us
  local copies, waits for them, and re-layouts: 8.5 us -> 6.22 us
  Pallas kernels: 27.3 us -> 29.1 us
    all_to_all x3, waiting for transfers between devices: 24.1 us -> 13.9 us  [swap_all(): return lax.all_to_all(value, REP, 0, 0, tiled=True)]
    all_to_all x1, blocking collectives: 16.3 us -> 24.8 us  [swap_all(): return lax.all_to_all(value, REP, 0, 0, tiled=True)]
    unnamed x34 -> x20, local copies, waits for them, and re-layouts: 6.51 us -> 3.33 us
    pallas_call x1 -> x2, Pallas kernels: 17.2 us -> 19.7 us  [project(): pl.pallas_call(functools.partial(project_kernel, slots), in_specs=smem(2)...]
    all_to_all x3, starting transfers between devices: 30.1 us -> 28 us  [swap_all(): return lax.all_to_all(value, REP, 0, 0, tiled=True)]
    pallas_call x2, Pallas kernels: 2.12 us -> 0.14 us  [pack(): pl.pallas_call(pack_kernel, in_specs=vmem(len(parts)), out_specs=pl.Block...]
  transfers between devices with their start and end apart: 22 -> 22, of which waited for: 5 -> 5; matrix products, arithmetic and copies ran while one was open for 1% -> 2% of each run, Pallas kernels for 16% -> 17%
where the time goes in v3:
time: 155 us
  starting transfers between devices  50.3 us (32%)
  Pallas kernels  29.1 us (19%)
  blocking collectives  24.8 us (16%)
  waiting for transfers between devices  24.7 us (16%)
  between operations  16.8 us (11%)
  local copies, waits for them, and re-layouts  6.22 us (4%)
  other arithmetic  2.55 us (2%)
    all_to_all x3, starting transfers between devices, swap_all(): return lax.all_to_all(value, REP, 0, 0, tiled=True)  28 us
    all_to_all x1, blocking collectives, swap_all(): return lax.all_to_all(value, REP, 0, 0, tiled=True)  24.8 us
    ppermute x18, starting transfers between devices, ring(): return lax.ppermute(value, axes, pairs)  22.2 us
    pallas_call x2, Pallas kernels, project(): pl.pallas_call(functools.partial(project_kernel, slots), in_specs=smem(2)...  19.7 us
    all_to_all x3, waiting for transfers between devices, swap_all(): return lax.all_to_all(value, REP, 0, 0, tiled=True)  13.9 us
    ppermute x18, waiting for transfers between devices, ring(): return lax.ppermute(value, axes, pairs)  10.8 us
    pallas_call x1, Pallas kernels, decode(): pl.pallas_call(decode_kernel, in_specs=smem(2) + vmem(1) + anywhere(2), o...  4.66 us
    unnamed x20, local copies, waits for them, and re-layouts  3.33 us
  transfers between devices with their start and end apart: 22, of which 5 were waited for; matrix products, arithmetic and copies ran while one was open for 2% of the time, Pallas kernels for 17%

profile of v3, /device:TPU:1, one launch (start us, length us, event | category | flops | bytes accessed | tf_op | source)
XLA Modules:
  0.0 154.5 jit_solution(10044649782149544367)
XLA Ops:
  7.2 0.0 all-gather.3.cloned.1.call-start
  7.3 1.1 fusion.1
  8.4 2.2 %collective-permute-start.2 = (bf16[128,1024]{1,0:T(8,128)(2,1)S(1)}, bf16[128,1024]{1,0:T(8,128)(2,1)S(1)}, u32[]{:S(2)}, u32[]{:S(2)}) collective-permute-start(bf16[128,1024]{1,0:T(8,128)(2,1)S(1)} %get-tuple-element.32.refs_0_), channel_id=1, source_target_pairs={{0,1},{1,2},{2,3},{3,0},{4,5},{5,6},{6,7},{7,4},{8,9},{9,10},{10,1... | collective-permute-start | bytes 786440 | tf_op jit(solution)/shard_map/ppermute | solution.py:38
  10.6 1.5 collective-permute-start.3
  12.1 0.1 pad_add_fusion.1.place_ref
  12.2 1.0 copy-done
  13.2 0.9 copy-done.2
  14.1 0.7 split.1
  14.8 1.3 collective-permute-start
  16.1 0.7 fusion
  19.3 2.5 %collective-permute-start.1 = (bf16[48,256]{1,0:T(8,128)(2,1)S(1)}, bf16[48,256]{1,0:T(8,128)(2,1)S(1)}, u32[]{:S(2)}, u32[]{:S(2)}) collective-permute-start(bf16[48,256]{1,0:T(8,128)(2,1)S(1)} %dynamic-slice_select_fusion), channel_id=1, source_target_pairs={{0,4},{4,0},{1,5},{5,1},{2,6},{6,2},{3,7},{7,3},{8,12},{12,8},{9,1... | collective-permute-start | bytes 73736 | tf_op jit(solution)/shard_map/ppermute | solution.py:38
  21.8 3.6 %collective-permute-done.1 = bf16[48,256]{1,0:T(8,128)(2,1)S(1)} collective-permute-done((bf16[48,256]{1,0:T(8,128)(2,1)S(1)}, bf16[48,256]{1,0:T(8,128)(2,1)S(1)}, u32[]{:S(2)}, u32[]{:S(2)}) %collective-permute-start.1) | collective-permute-done | bytes 24608 | tf_op jit(solution)/shard_map/ppermute | solution.py:38
  25.5 0.9 pad_maximum_fusion
  26.4 1.5 collective-permute-start.6
  27.9 0.8 collective-permute-start.5
  28.7 2.7 %collective-permute-start.8 = (bf16[128,1024]{1,0:T(8,128)(2,1)S(1)}, bf16[128,1024]{1,0:T(8,128)(2,1)S(1)}, u32[]{:S(2)}, u32[]{:S(2)}) collective-permute-start(bf16[128,1024]{1,0:T(8,128)(2,1)S(1)} %get-tuple-element.28.refs_0_), channel_id=1, source_target_pairs={{0,132},{128,0},{4,128},{132,4},{1,133},{129,1},{5,129},{133,5},{2... | collective-permute-start | bytes 786440 | tf_op jit(solution)/shard_map/ppermute | solution.py:38
  31.4 1.4 collective-permute-start.10
  32.8 0.2 collective-permute-start.4
  33.0 5.6 %collective-permute-done.4 = bf16[48,256]{1,0:T(8,128)(2,1)S(1)} collective-permute-done((bf16[48,256]{1,0:T(8,128)(2,1)S(1)}, bf16[48,256]{1,0:T(8,128)(2,1)S(1)}, u32[]{:S(2)}, u32[]{:S(2)}) %collective-permute-start.4) | collective-permute-done | bytes 24608 | tf_op jit(solution)/shard_map/ppermute | solution.py:38
  38.7 0.9 decode_partial.1
  39.7 1.5 %collective-permute-done.9.refs_3_ = bf16[128,1024]{1,0:T(8,128)(2,1)S(1)} collective-permute-done((bf16[128,1024]{1,0:T(8,128)(2,1)S(1)}, bf16[128,1024]{1,0:T(8,128)(2,1)S(1)}, u32[]{:S(2)}, u32[]{:S(2)}) %collective-permute-start.9) | collective-permute-done | bytes 262176 | tf_op jit(solution)/shard_map/ppermute | solution.py:38
  41.2 0.1 pack.3.refs_4_
  41.3 0.1 collective-permute-start.14
  41.4 2.7 %collective-permute-start.15 = (bf16[512,1024]{1,0:T(8,128)(2,1)S(1)}, bf16[512,1024]{1,0:T(8,128)(2,1)}, u32[]{:S(2)}, u32[]{:S(2)}) collective-permute-start(bf16[512,1024]{1,0:T(8,128)(2,1)S(1)} %pack.3.refs_4_), channel_id=1, source_target_pairs={{0,132},{128,0},{4,128},{132,4},{1,133},{129,1},{5,129},{133,5},{2... | collective-permute-start | bytes 3145736 | tf_op jit(solution)/shard_map/ppermute | solution.py:38
  44.0 12.6 %all-to-all-start = ((f32[64,8,128]{2,1,0:T(8,128)}), f32[64,8,128]{2,1,0:T(8,128)S(1)}, u32[]{:S(2)}, u32[]{:S(2)}) async-start(f32[64,8,128]{2,1,0:T(8,128)} %decode_partial.1), calls=%async_computation | async-start | bytes 524288 | tf_op jit(solution)/shard_map/all_to_all | solution.py:331
  56.7 0.1 pack.2.refs_0_
  56.8 0.8 collective-permute-start.11
  57.5 2.0 %collective-permute-start.12 = (bf16[512,1024]{1,0:T(8,128)(2,1)S(1)}, bf16[512,1024]{1,0:T(8,128)(2,1)}, u32[]{:S(2)}, u32[]{:S(2)}) collective-permute-start(bf16[512,1024]{1,0:T(8,128)(2,1)S(1)} %pack.2.refs_0_), channel_id=1, source_target_pairs={{0,3},{1,0},{2,1},{3,2},{4,7},{5,4},{6,5},{7,6},{8,11},{9,8},{10,9... | collective-permute-start | bytes 3145736 | tf_op jit(solution)/shard_map/ppermute | solution.py:38
  59.5 0.2 collective-permute-start.13
  59.7 11.6 %all-to-all-done = f32[64,8,128]{2,1,0:T(8,128)S(1)} async-done(((f32[64,8,128]{2,1,0:T(8,128)}), f32[64,8,128]{2,1,0:T(8,128)S(1)}, u32[]{:S(2)}, u32[]{:S(2)}) %all-to-all-start) | async-done | bytes 262176 | tf_op jit(solution)/shard_map/all_to_all | solution.py:331
  71.3 2.0 %collective-permute-start.16 = (bf16[512,1024]{1,0:T(8,128)(2,1)S(1)}, bf16[512,1024]{1,0:T(8,128)(2,1)}, u32[]{:S(2)}, u32[]{:S(2)}) collective-permute-start(bf16[512,1024]{1,0:T(8,128)(2,1)S(1)} %pack.3.refs_4_), channel_id=1, source_target_pairs={{0,4},{128,132},{4,0},{132,128},{1,5},{129,133},{5,1},{133,129},{2... | collective-permute-start | bytes 3145736 | tf_op jit(solution)/shard_map/ppermute | solution.py:38
  73.4 24.8 %all_to_all.20.tile_ref = bf16[32,16,128]{2,1,0:T(8,128)(2,1)} all-to-all(bf16[32,16,128]{2,1,0:T(8,128)(2,1)S(1)} %decode_total.1), channel_id=1, replica_groups=mesh['xl'=2,'z'=8,'c'=2,'xh'=2,'y'=4] {'xl','z','c'}, dimensions={0} | all-to-all | bytes 262144 | tf_op jit(solution)/shard_map/all_to_all | solution.py:331
  98.2 4.7 %decode_attention.1 = f32[32,24,128]{2,1,0:T(8,128)} custom-call(s32[4]{0:T(128)} %copy-done.6, s32[48]{0:T(128)} %length_ref.1, bf16[32,16,128]{2,1,0:T(8,128)(2,1)} %all_to_all.20.tile_ref, bf16[48,128,128]{2,1,0:T(8,128)(2,1)} %key_hbm.1, bf16[48,128,128]{2,1,0:T(8,128)(2,1)} %value_hbm.1), custom_call_target="tpu_custom_call" | custom-call | flops 30000000 | bytes 4000000 | tf_op jit(solution)/shard_map/decode_attention/pallas_call | solution.py:288
  102.9 9.1 %all-to-all-start.2 = ((f32[32,24,128]{2,1,0:T(8,128)}), f32[32,24,128]{2,1,0:T(8,128)S(1)}, u32[]{:S(2)}, u32[]{:S(2)}) async-start(f32[32,24,128]{2,1,0:T(8,128)} %decode_attention.1), calls=%async_computation.2 | async-start | bytes 786432 | tf_op jit(solution)/shard_map/all_to_all | solution.py:331
  112.0 0.1 copy.11
  112.1 0.1 eq.27
  112.2 0.8 select_reduce_fusion.logical_ref
  113.1 10.0 %project.3 = bf16[256,640]{1,0:T(8,128)(2,1)S(1)} custom-call(s32[4]{0:T(128)S(1)} %copy-done.7, s32[32]{0:T(128)S(1)} %select_reduce_fusion.logical_ref, bf16[512,1024]{1,0:T(8,128)(2,1)S(1)} %pack.2.refs_0_, bf16[512,1024]{1,0:T(8,128)(2,1)S(1)} %collective-permute-done.11.refs_1_, bf16[512,1024]{1,0:T(8,128)(2,1)} %collective-permute-done.12.refs_2_, ...), custom_call_target="tpu_custom_call" | custom-call | flops 2684354560 | bytes 15000000 | tf_op jit(solution)/shard_map/project/pallas_call | solution.py:154
  123.1 0.7 copy-done.5
  123.8 2.3 %all-to-all-done.2.in_ref = f32[32,24,128]{2,1,0:T(8,128)S(1)} async-done(((f32[32,24,128]{2,1,0:T(8,128)}), f32[32,24,128]{2,1,0:T(8,128)S(1)}, u32[]{:S(2)}, u32[]{:S(2)}) %all-to-all-start.2) | async-done | bytes 393248 | tf_op jit(solution)/shard_map/all_to_all | solution.py:331
  126.1 0.3 collective-permute-start.17
  126.4 0.3 decode_combine.1
  126.7 0.6 copy-done.4
  127.3 6.3 %all-to-all-start.3 = ((bf16[32,16,128]{2,1,0:T(8,128)(2,1)}), bf16[32,16,128]{2,1,0:T(8,128)(2,1)}, u32[]{:S(2)}, u32[]{:S(2)}) async-start(bf16[32,16,128]{2,1,0:T(8,128)(2,1)} %copy-done.4), calls=%async_computation.3 | async-start | bytes 262144 | tf_op jit(solution)/shard_map/all_to_all | solution.py:331
  133.7 9.7 %project.2.mine_ref = bf16[256,640]{1,0:T(8,128)(2,1)S(1)} custom-call(s32[4]{0:T(128)S(1)} %copy-done.7, s32[32]{0:T(128)S(1)} %select_reduce_fusion.logical_ref, bf16[512,1024]{1,0:T(8,128)(2,1)S(1)} %pack.2.refs_0_, bf16[512,1024]{1,0:T(8,128)(2,1)S(1)} %collective-permute-done.11.refs_1_, bf16[512,1024]{1,0:T(8,128)(2,1)} %collective-permute-done.12.refs_2_, ...), custom_call_target="tpu_custom_call" | custom-call | flops 2684354560 | bytes 15000000 | tf_op jit(solution)/shard_map/project/pallas_call | solution.py:154
  143.4 0.9 slice.12
  144.3 0.7 reshape.31
  145.0 2.6 %prefill_attention.1 = bf16[256,1024]{1,0:T(8,128)(2,1)} custom-call(s32[4]{0:T(128)S(1)} %copy-done.7, bf16[256,640]{1,0:T(8,128)(2,1)S(1)} %project.2.mine_ref, bf16[256,640]{1,0:T(8,128)(2,1)} %collective-permute-done.17.other_ref), custom_call_target="tpu_custom_call" | custom-call | flops 140000000 | bytes 1200000 | tf_op jit(solution)/shard_map/prefill_attention/pallas_call | solution.py:197
  (43 shorter events, 0.2 us)
Async XLA Ops:
  7.2 8.9 %copy-start.9 = (s32[32]{0:T(128)S(1)}, s32[32]{0:T(128)}, u32[]{:S(2)}) copy-start(s32[32]{0:T(128)} %param.15) | copy-start | bytes 388
  7.2 12.1 %copy-start.8 = (bf16[48,1024]{1,0:T(8,128)(2,1)S(1)}, bf16[48,1024]{1,0:T(8,128)(2,1)}, u32[]{:S(2)}) copy-start(bf16[48,1024]{1,0:T(8,128)(2,1)} %param.9) | copy-start | bytes 294916
  7.2 105.9 %all-gather.3.cloned.1.call-start = ((), (), s32[]{:S(2)}) async-start(), calls=%async_computation.4 | async-start | bytes 11141120 | tf_op jit(solution)/shard_map/all_gather | solution.py:352
  7.2 31.5 %copy-start.1 = (bf16[256,1024]{1,0:T(8,128)(2,1)S(1)}, bf16[256,1024]{1,0:T(8,128)(2,1)}, u32[]{:S(2)}) copy-start(bf16[256,1024]{1,0:T(8,128)(2,1)} %qw_ref.3) | copy-start | bytes 1572868
  7.2 31.5 %copy-start.3 = (bf16[256,256]{1,0:T(8,128)(2,1)S(1)}, bf16[256,256]{1,0:T(8,128)(2,1)}, u32[]{:S(2)}) copy-start(bf16[256,256]{1,0:T(8,128)(2,1)} %kv_ref.3) | copy-start | bytes 393220
  8.4 17.1 %collective-permute-start.2 = (bf16[128,1024]{1,0:T(8,128)(2,1)S(1)}, bf16[128,1024]{1,0:T(8,128)(2,1)S(1)}, u32[]{:S(2)}, u32[]{:S(2)}) collective-permute-start(bf16[128,1024]{1,0:T(8,128)(2,1)S(1)} %get-tuple-element.32.refs_0_), channel_id=1, source_target_pairs={{0,1},{1,2},{2,3},{3,0},{4,5},{5,6},{6,7},{7,4},{8,9},{9,10},{10,1... | collective-permute-start | bytes 786440 | tf_op jit(solution)/shard_map/ppermute | solution.py:38
  10.6 14.9 %collective-permute-start.3 = (bf16[128,1024]{1,0:T(8,128)(2,1)S(1)}, bf16[128,1024]{1,0:T(8,128)(2,1)S(1)}, u32[]{:S(2)}, u32[]{:S(2)}) collective-permute-start(bf16[128,1024]{1,0:T(8,128)(2,1)S(1)} %get-tuple-element.32.refs_0_), channel_id=1, source_target_pairs={{0,3},{1,0},{2,1},{3,2},{4,7},{5,4},{6,5},{7,6},{8,11},{9,8},{10,9... | collective-permute-start | bytes 786440 | tf_op jit(solution)/shard_map/ppermute | solution.py:38
  12.2 1.0 copy-start
  13.2 0.9 copy-start.2
  14.1 25.5 %copy-start.6 = (s32[4]{0:T(128)}, s32[4]{0:T(128)S(1)}, u32[]{:S(2)}) copy-start(s32[4]{0:T(128)S(1)} %pad_add_fusion.1.place_ref) | copy-start | bytes 52
  14.8 10.7 %collective-permute-start = (bf16[256,640]{1,0:T(8,128)(2,1)S(1)}, bf16[256,640]{1,0:T(8,128)(2,1)S(1)}, u32[]{:S(2)}, u32[]{:S(2)}) collective-permute-start(bf16[256,640]{1,0:T(8,128)(2,1)S(1)} %get-tuple-element.24), channel_id=1, source_target_pairs={{0,128},{128,0},{1,129},{129,1},{2,130},{130,2},{3,131},{131,3},{4... | collective-permute-start | bytes 983048 | tf_op jit(solution)/shard_map/ppermute | solution.py:38
  19.3 6.2 %collective-permute-start.1 = (bf16[48,256]{1,0:T(8,128)(2,1)S(1)}, bf16[48,256]{1,0:T(8,128)(2,1)S(1)}, u32[]{:S(2)}, u32[]{:S(2)}) collective-permute-start(bf16[48,256]{1,0:T(8,128)(2,1)S(1)} %dynamic-slice_select_fusion), channel_id=1, source_target_pairs={{0,4},{4,0},{1,5},{5,1},{2,6},{6,2},{3,7},{7,3},{8,12},{12,8},{9,1... | collective-permute-start | bytes 73736 | tf_op jit(solution)/shard_map/ppermute | solution.py:38
  26.4 4.9 %collective-permute-start.6 = (bf16[48,256]{1,0:T(8,128)(2,1)S(1)}, bf16[48,256]{1,0:T(8,128)(2,1)S(1)}, u32[]{:S(2)}, u32[]{:S(2)}) collective-permute-start(bf16[48,256]{1,0:T(8,128)(2,1)S(1)} %fusion.2), channel_id=1, source_target_pairs={{0,2},{1,3},{2,0},{3,1},{4,6},{5,7},{6,4},{7,5},{8,10},{9,11},{10,... | collective-permute-start | bytes 73736 | tf_op jit(solution)/shard_map/ppermute | solution.py:38
  27.9 4.9 %collective-permute-start.5 = (bf16[48,256]{1,0:T(8,128)(2,1)S(1)}, bf16[48,256]{1,0:T(8,128)(2,1)S(1)}, u32[]{:S(2)}, u32[]{:S(2)}) collective-permute-start(bf16[48,256]{1,0:T(8,128)(2,1)S(1)} %fusion.2), channel_id=1, source_target_pairs={{0,3},{1,0},{2,1},{3,2},{4,7},{5,4},{6,5},{7,6},{8,11},{9,8},{10,9... | collective-permute-start | bytes 73736 | tf_op jit(solution)/shard_map/ppermute | solution.py:38
  28.7 11.0 %collective-permute-start.7 = (bf16[128,1024]{1,0:T(8,128)(2,1)S(1)}, bf16[128,1024]{1,0:T(8,128)(2,1)S(1)}, u32[]{:S(2)}, u32[]{:S(2)}) collective-permute-start(bf16[128,1024]{1,0:T(8,128)(2,1)S(1)} %get-tuple-element.28.refs_0_), channel_id=1, source_target_pairs={{0,128},{128,4},{4,132},{132,0},{1,129},{129,5},{5,133},{133,1},{2... | collective-permute-start | bytes 786440 | tf_op jit(solution)/shard_map/ppermute | solution.py:38
  28.7 11.0 %collective-permute-start.8 = (bf16[128,1024]{1,0:T(8,128)(2,1)S(1)}, bf16[128,1024]{1,0:T(8,128)(2,1)S(1)}, u32[]{:S(2)}, u32[]{:S(2)}) collective-permute-start(bf16[128,1024]{1,0:T(8,128)(2,1)S(1)} %get-tuple-element.28.refs_0_), channel_id=1, source_target_pairs={{0,132},{128,0},{4,128},{132,4},{1,133},{129,1},{5,129},{133,5},{2... | collective-permute-start | bytes 786440 | tf_op jit(solution)/shard_map/ppermute | solution.py:38
  31.4 9.8 %collective-permute-start.9 = (bf16[128,1024]{1,0:T(8,128)(2,1)S(1)}, bf16[128,1024]{1,0:T(8,128)(2,1)S(1)}, u32[]{:S(2)}, u32[]{:S(2)}) collective-permute-start(bf16[128,1024]{1,0:T(8,128)(2,1)S(1)} %get-tuple-element.28.refs_0_), channel_id=1, source_target_pairs={{0,4},{128,132},{4,0},{132,128},{1,5},{129,133},{5,1},{133,129},{2... | collective-permute-start | bytes 786440 | tf_op jit(solution)/shard_map/ppermute | solution.py:38
  31.4 9.8 %collective-permute-start.10 = (bf16[128,1024]{1,0:T(8,128)(2,1)S(1)}, bf16[128,1024]{1,0:T(8,128)(2,1)S(1)}, u32[]{:S(2)}, u32[]{:S(2)}) collective-permute-start(bf16[128,1024]{1,0:T(8,128)(2,1)S(1)} %get-tuple-element.32.refs_0_), channel_id=1, source_target_pairs={{0,2},{1,3},{2,0},{3,1},{4,6},{5,7},{6,4},{7,5},{8,10},{9,11},{10,... | collective-permute-start | bytes 786440 | tf_op jit(solution)/shard_map/ppermute | solution.py:38
  32.8 5.9 %collective-permute-start.4 = (bf16[48,256]{1,0:T(8,128)(2,1)S(1)}, bf16[48,256]{1,0:T(8,128)(2,1)S(1)}, u32[]{:S(2)}, u32[]{:S(2)}) collective-permute-start(bf16[48,256]{1,0:T(8,128)(2,1)S(1)} %fusion.2), channel_id=1, source_target_pairs={{0,1},{1,2},{2,3},{3,0},{4,5},{5,6},{6,7},{7,4},{8,9},{9,10},{10,1... | collective-permute-start | bytes 73736 | tf_op jit(solution)/shard_map/ppermute | solution.py:38
  41.3 30.0 %collective-permute-start.14 = (bf16[512,1024]{1,0:T(8,128)(2,1)S(1)}, bf16[512,1024]{1,0:T(8,128)(2,1)}, u32[]{:S(2)}, u32[]{:S(2)}) collective-permute-start(bf16[512,1024]{1,0:T(8,128)(2,1)S(1)} %pack.3.refs_4_), channel_id=1, source_target_pairs={{0,128},{128,4},{4,132},{132,0},{1,129},{129,5},{5,133},{133,1},{2... | collective-permute-start | bytes 3145736 | tf_op jit(solution)/shard_map/ppermute | solution.py:38
  41.4 29.9 %collective-permute-start.15 = (bf16[512,1024]{1,0:T(8,128)(2,1)S(1)}, bf16[512,1024]{1,0:T(8,128)(2,1)}, u32[]{:S(2)}, u32[]{:S(2)}) collective-permute-start(bf16[512,1024]{1,0:T(8,128)(2,1)S(1)} %pack.3.refs_4_), channel_id=1, source_target_pairs={{0,132},{128,0},{4,128},{132,4},{1,133},{129,1},{5,129},{133,5},{2... | collective-permute-start | bytes 3145736 | tf_op jit(solution)/shard_map/ppermute | solution.py:38
  44.0 27.2 %all-to-all-start = ((f32[64,8,128]{2,1,0:T(8,128)}), f32[64,8,128]{2,1,0:T(8,128)S(1)}, u32[]{:S(2)}, u32[]{:S(2)}) async-start(f32[64,8,128]{2,1,0:T(8,128)} %decode_partial.1), calls=%async_computation | async-start | bytes 524288 | tf_op jit(solution)/shard_map/all_to_all | solution.py:331
  56.8 56.3 %collective-permute-start.11 = (bf16[512,1024]{1,0:T(8,128)(2,1)S(1)}, bf16[512,1024]{1,0:T(8,128)(2,1)S(1)}, u32[]{:S(2)}, u32[]{:S(2)}) collective-permute-start(bf16[512,1024]{1,0:T(8,128)(2,1)S(1)} %pack.2.refs_0_), channel_id=1, source_target_pairs={{0,1},{1,2},{2,3},{3,0},{4,5},{5,6},{6,7},{7,4},{8,9},{9,10},{10,1... | collective-permute-start | bytes 3145736 | tf_op jit(solution)/shard_map/ppermute | solution.py:38
  57.5 55.5 %collective-permute-start.12 = (bf16[512,1024]{1,0:T(8,128)(2,1)S(1)}, bf16[512,1024]{1,0:T(8,128)(2,1)}, u32[]{:S(2)}, u32[]{:S(2)}) collective-permute-start(bf16[512,1024]{1,0:T(8,128)(2,1)S(1)} %pack.2.refs_0_), channel_id=1, source_target_pairs={{0,3},{1,0},{2,1},{3,2},{4,7},{5,4},{6,5},{7,6},{8,11},{9,8},{10,9... | collective-permute-start | bytes 3145736 | tf_op jit(solution)/shard_map/ppermute | solution.py:38
  59.5 53.5 %collective-permute-start.13 = (bf16[512,1024]{1,0:T(8,128)(2,1)S(1)}, bf16[512,1024]{1,0:T(8,128)(2,1)}, u32[]{:S(2)}, u32[]{:S(2)}) collective-permute-start(bf16[512,1024]{1,0:T(8,128)(2,1)S(1)} %pack.2.refs_0_), channel_id=1, source_target_pairs={{0,2},{1,3},{2,0},{3,1},{4,6},{5,7},{6,4},{7,5},{8,10},{9,11},{10,... | collective-permute-start | bytes 3145736 | tf_op jit(solution)/shard_map/ppermute | solution.py:38
  71.3 41.7 %collective-permute-start.16 = (bf16[512,1024]{1,0:T(8,128)(2,1)S(1)}, bf16[512,1024]{1,0:T(8,128)(2,1)}, u32[]{:S(2)}, u32[]{:S(2)}) collective-permute-start(bf16[512,1024]{1,0:T(8,128)(2,1)S(1)} %pack.3.refs_4_), channel_id=1, source_target_pairs={{0,4},{128,132},{4,0},{132,128},{1,5},{129,133},{5,1},{133,129},{2... | collective-permute-start | bytes 3145736 | tf_op jit(solution)/shard_map/ppermute | solution.py:38
  98.2 14.9 %copy-start.7 = (s32[4]{0:T(128)S(1)}, s32[4]{0:T(128)}, u32[]{:S(2)}) copy-start(s32[4]{0:T(128)} %copy-done.6) | copy-start | bytes 52
  102.9 23.2 %all-to-all-start.2 = ((f32[32,24,128]{2,1,0:T(8,128)}), f32[32,24,128]{2,1,0:T(8,128)S(1)}, u32[]{:S(2)}, u32[]{:S(2)}) async-start(f32[32,24,128]{2,1,0:T(8,128)} %decode_attention.1), calls=%async_computation.2 | async-start | bytes 786432 | tf_op jit(solution)/shard_map/all_to_all | solution.py:331
  123.1 0.7 copy-start.5
  126.1 19.0 %collective-permute-start.17 = (bf16[256,640]{1,0:T(8,128)(2,1)}, bf16[256,640]{1,0:T(8,128)(2,1)}, u32[]{:S(2)}, u32[]{:S(2)}) collective-permute-start(bf16[256,640]{1,0:T(8,128)(2,1)} %copy-done.5), channel_id=1, source_target_pairs={{0,128},{128,0},{1,129},{129,1},{2,130},{130,2},{3,131},{131,3},{4... | collective-permute-start | bytes 983048 | tf_op jit(solution)/shard_map/ppermute | solution.py:38
  126.7 0.7 copy-start.4
  127.3 16.1 %all-to-all-start.3 = ((bf16[32,16,128]{2,1,0:T(8,128)(2,1)}), bf16[32,16,128]{2,1,0:T(8,128)(2,1)}, u32[]{:S(2)}, u32[]{:S(2)}) async-start(bf16[32,16,128]{2,1,0:T(8,128)(2,1)} %copy-done.4), calls=%async_computation.3 | async-start | bytes 262144 | tf_op jit(solution)/shard_map/all_to_all | solution.py:331
Sparse Core Ops, SparseCore 0:
  26.6 76.0 all-gather.2

commit v4 on v3

--- a/solution.py
+++ b/solution.py
@@ -169,7 +169,10 @@
     )(place, logical, *a, *b, w)
 
 
-def prefill_kernel(place_ref, mine_ref, other_ref, out_ref):
+def prefill_kernel(place_ref, mine_ref, other_ref, decode_ref, out_ref, decode_out_ref, rows_ref):
+    rows_ref[...] = decode_ref[: BATCH // 2].astype(f32).reshape(BATCH, HEADS, HD)
+    for head in range(HEADS):
+        decode_out_ref[:, head * HD : (head + 1) * HD] = rows_ref[:, head, :].astype(decode_out_ref.dtype)
     first = place_ref[0] == 0
     mine, other = mine_ref[...], other_ref[...]
     low = jnp.where(first, mine, other)
@@ -193,16 +196,17 @@
             out_ref[at, head * HD : (head + 1) * HD] = weighted[head * SEQ_LEN : (head + 1) * SEQ_LEN]
 
 
-def prefill(place, mine, other):
+def prefill(place, mine, other, decoded):
     return pl.pallas_call(
         prefill_kernel,
-        in_specs=smem(1) + vmem(2),
-        out_specs=pl.BlockSpec(memory_space=pltpu.VMEM),
-        out_shape=bf16(ROWS, WIDTH),
+        in_specs=smem(1) + vmem(3),
+        out_specs=vmem(2),
+        out_shape=[bf16(ROWS, WIDTH), bf16(BATCH, WIDTH)],
+        scratch_shapes=[pltpu.VMEM((BATCH, HEADS, HD), f32)],
         compiler_params=params(),
         cost_estimate=pl.CostEstimate(flops=140_000_000, bytes_accessed=1_200_000, transcendentals=262144),
         name="prefill_attention",
-    )(place, mine, other)
+    )(place, mine, other, decoded)
 
 
 def partial_kernel(x_ref, qw_ref, kv_ref, out_ref):
@@ -375,8 +379,7 @@
     other = ring(theirs, "xl", 2, 1)
     done = combine(parts)
     mine = project(OWN, place, logical, xa, xb, weights)
-    attn_pre = prefill(place, mine, other)
-    attn_dec = swap_all(done)[: BATCH // 2].reshape(BATCH, WIDTH)
+    attn_pre, attn_dec = prefill(place, mine, other, swap_all(done))
     return attn_pre, attn_dec
 
 

time: 155 us -> 154 us (level)
  local copies, waits for them, and re-layouts: 6.22 us -> 4.63 us
  transfers between devices with their start and end apart: 22 -> 22, of which waited for: 5 -> 5; matrix products, arithmetic and copies ran while one was open for 2% -> 1% of each run, Pallas kernels for 17% -> 17%
where the time goes in v4:
time: 154 us; the launch traced here: 153 us
  starting transfers between devices  50.3 us (33%)
  Pallas kernels  29.1 us (19%)
  blocking collectives  24.8 us (16%)
  waiting for transfers between devices  24.7 us (16%)
  between operations  16.8 us (11%)
  local copies, waits for them, and re-layouts  4.63 us (3%)
  other arithmetic  2.55 us (2%)
    all_to_all x3, starting transfers between devices, swap_all(): return lax.all_to_all(value, REP, 0, 0, tiled=True)  28 us
    all_to_all x1, blocking collectives, swap_all(): return lax.all_to_all(value, REP, 0, 0, tiled=True)  24.8 us
    ppermute x18, starting transfers between devices, ring(): return lax.ppermute(value, axes, pairs)  22.2 us
    pallas_call x2, Pallas kernels, project(): pl.pallas_call(functools.partial(project_kernel, slots), in_specs=smem(2)...  19.7 us
    all_to_all x3, waiting for transfers between devices, swap_all(): return lax.all_to_all(value, REP, 0, 0, tiled=True)  13.8 us
    ppermute x18, waiting for transfers between devices, ring(): return lax.ppermute(value, axes, pairs)  10.8 us
    pallas_call x1, Pallas kernels, decode(): pl.pallas_call(decode_kernel, in_specs=smem(2) + vmem(1) + anywhere(2), o...  4.66 us
    unnamed x20, local copies, waits for them, and re-layouts  3.33 us
  transfers between devices with their start and end apart: 22, of which 5 were waited for; matrix products, arithmetic and copies ran while one was open for 1% of the time, Pallas kernels for 17%

profile of v4, /device:TPU:1, one launch (start us, length us, event | category | flops | bytes accessed | tf_op | source)
XLA Modules:
  0.0 153.0 jit_solution(8208769580677075345)
XLA Ops:
  7.2 0.0 all-gather.3.cloned.1.call-start
  7.3 1.1 fusion.1
  8.4 2.2 %collective-permute-start.2 = (bf16[128,1024]{1,0:T(8,128)(2,1)S(1)}, bf16[128,1024]{1,0:T(8,128)(2,1)S(1)}, u32[]{:S(2)}, u32[]{:S(2)}) collective-permute-start(bf16[128,1024]{1,0:T(8,128)(2,1)S(1)} %get-tuple-element.32.refs_0_), channel_id=1, source_target_pairs={{0,1},{1,2},{2,3},{3,0},{4,5},{5,6},{6,7},{7,4},{8,9},{9,10},{10,1... | collective-permute-start | bytes 786440 | tf_op jit(solution)/shard_map/ppermute | solution.py:38
  10.6 1.5 collective-permute-start.3
  12.1 0.1 pad_add_fusion.1.place_ref
  12.2 1.0 copy-done
  13.2 0.9 copy-done.2
  14.1 0.7 split.1
  14.8 1.3 collective-permute-start
  16.1 0.7 fusion
  19.3 2.5 %collective-permute-start.1 = (bf16[48,256]{1,0:T(8,128)(2,1)S(1)}, bf16[48,256]{1,0:T(8,128)(2,1)S(1)}, u32[]{:S(2)}, u32[]{:S(2)}) collective-permute-start(bf16[48,256]{1,0:T(8,128)(2,1)S(1)} %dynamic-slice_select_fusion), channel_id=1, source_target_pairs={{0,4},{4,0},{1,5},{5,1},{2,6},{6,2},{3,7},{7,3},{8,12},{12,8},{9,1... | collective-permute-start | bytes 73736 | tf_op jit(solution)/shard_map/ppermute | solution.py:38
  21.8 3.6 %collective-permute-done.1 = bf16[48,256]{1,0:T(8,128)(2,1)S(1)} collective-permute-done((bf16[48,256]{1,0:T(8,128)(2,1)S(1)}, bf16[48,256]{1,0:T(8,128)(2,1)S(1)}, u32[]{:S(2)}, u32[]{:S(2)}) %collective-permute-start.1) | collective-permute-done | bytes 24608 | tf_op jit(solution)/shard_map/ppermute | solution.py:38
  25.5 0.9 pad_maximum_fusion
  26.4 0.0 all-gather.3.cloned.1.call-update
  26.4 1.5 collective-permute-start.6
  27.9 0.8 collective-permute-start.5
  28.7 2.7 %collective-permute-start.8 = (bf16[128,1024]{1,0:T(8,128)(2,1)S(1)}, bf16[128,1024]{1,0:T(8,128)(2,1)S(1)}, u32[]{:S(2)}, u32[]{:S(2)}) collective-permute-start(bf16[128,1024]{1,0:T(8,128)(2,1)S(1)} %get-tuple-element.28.refs_0_), channel_id=1, source_target_pairs={{0,132},{128,0},{4,128},{132,4},{1,133},{129,1},{5,129},{133,5},{2... | collective-permute-start | bytes 786440 | tf_op jit(solution)/shard_map/ppermute | solution.py:38
  31.4 1.4 collective-permute-start.10
  32.8 0.2 collective-permute-start.4
  33.0 5.6 %collective-permute-done.4 = bf16[48,256]{1,0:T(8,128)(2,1)S(1)} collective-permute-done((bf16[48,256]{1,0:T(8,128)(2,1)S(1)}, bf16[48,256]{1,0:T(8,128)(2,1)S(1)}, u32[]{:S(2)}, u32[]{:S(2)}) %collective-permute-start.4) | collective-permute-done | bytes 24608 | tf_op jit(solution)/shard_map/ppermute | solution.py:38
  38.7 0.9 decode_partial.1
  39.7 1.5 %collective-permute-done.9.refs_3_ = bf16[128,1024]{1,0:T(8,128)(2,1)S(1)} collective-permute-done((bf16[128,1024]{1,0:T(8,128)(2,1)S(1)}, bf16[128,1024]{1,0:T(8,128)(2,1)S(1)}, u32[]{:S(2)}, u32[]{:S(2)}) %collective-permute-start.9) | collective-permute-done | bytes 262176 | tf_op jit(solution)/shard_map/ppermute | solution.py:38
  41.2 0.1 pack.3.refs_4_
  41.3 0.1 collective-permute-start.14
  41.4 2.7 %collective-permute-start.15 = (bf16[512,1024]{1,0:T(8,128)(2,1)S(1)}, bf16[512,1024]{1,0:T(8,128)(2,1)}, u32[]{:S(2)}, u32[]{:S(2)}) collective-permute-start(bf16[512,1024]{1,0:T(8,128)(2,1)S(1)} %pack.3.refs_4_), channel_id=1, source_target_pairs={{0,132},{128,0},{4,128},{132,4},{1,133},{129,1},{5,129},{133,5},{2... | collective-permute-start | bytes 3145736 | tf_op jit(solution)/shard_map/ppermute | solution.py:38
  44.0 12.6 %all-to-all-start = ((f32[64,8,128]{2,1,0:T(8,128)}), f32[64,8,128]{2,1,0:T(8,128)S(1)}, u32[]{:S(2)}, u32[]{:S(2)}) async-start(f32[64,8,128]{2,1,0:T(8,128)} %decode_partial.1), calls=%async_computation | async-start | bytes 524288 | tf_op jit(solution)/shard_map/all_to_all | solution.py:335
  56.7 0.1 pack.2.refs_0_
  56.8 0.8 collective-permute-start.11
  57.5 2.0 %collective-permute-start.12 = (bf16[512,1024]{1,0:T(8,128)(2,1)S(1)}, bf16[512,1024]{1,0:T(8,128)(2,1)}, u32[]{:S(2)}, u32[]{:S(2)}) collective-permute-start(bf16[512,1024]{1,0:T(8,128)(2,1)S(1)} %pack.2.refs_0_), channel_id=1, source_target_pairs={{0,3},{1,0},{2,1},{3,2},{4,7},{5,4},{6,5},{7,6},{8,11},{9,8},{10,9... | collective-permute-start | bytes 3145736 | tf_op jit(solution)/shard_map/ppermute | solution.py:38
  59.5 0.2 collective-permute-start.13
  59.7 11.6 %all-to-all-done = f32[64,8,128]{2,1,0:T(8,128)S(1)} async-done(((f32[64,8,128]{2,1,0:T(8,128)}), f32[64,8,128]{2,1,0:T(8,128)S(1)}, u32[]{:S(2)}, u32[]{:S(2)}) %all-to-all-start) | async-done | bytes 262176 | tf_op jit(solution)/shard_map/all_to_all | solution.py:335
  71.3 2.1 %collective-permute-start.16 = (bf16[512,1024]{1,0:T(8,128)(2,1)S(1)}, bf16[512,1024]{1,0:T(8,128)(2,1)}, u32[]{:S(2)}, u32[]{:S(2)}) collective-permute-start(bf16[512,1024]{1,0:T(8,128)(2,1)S(1)} %pack.3.refs_4_), channel_id=1, source_target_pairs={{0,4},{128,132},{4,0},{132,128},{1,5},{129,133},{5,1},{133,129},{2... | collective-permute-start | bytes 3145736 | tf_op jit(solution)/shard_map/ppermute | solution.py:38
  73.4 24.8 %all_to_all.20.tile_ref = bf16[32,16,128]{2,1,0:T(8,128)(2,1)} all-to-all(bf16[32,16,128]{2,1,0:T(8,128)(2,1)S(1)} %decode_total.1), channel_id=1, replica_groups=mesh['xl'=2,'z'=8,'c'=2,'xh'=2,'y'=4] {'xl','z','c'}, dimensions={0} | all-to-all | bytes 262144 | tf_op jit(solution)/shard_map/all_to_all | solution.py:335
  98.2 4.7 %decode_attention.1 = f32[32,24,128]{2,1,0:T(8,128)} custom-call(s32[4]{0:T(128)} %copy-done.6, s32[48]{0:T(128)} %length_ref.1, bf16[32,16,128]{2,1,0:T(8,128)(2,1)} %all_to_all.20.tile_ref, bf16[48,128,128]{2,1,0:T(8,128)(2,1)} %key_hbm.1, bf16[48,128,128]{2,1,0:T(8,128)(2,1)} %value_hbm.1), custom_call_target="tpu_custom_call" | custom-call | flops 30000000 | bytes 4000000 | tf_op jit(solution)/shard_map/decode_attention/pallas_call | solution.py:292
  102.9 9.1 %all-to-all-start.2 = ((f32[32,24,128]{2,1,0:T(8,128)}), f32[32,24,128]{2,1,0:T(8,128)S(1)}, u32[]{:S(2)}, u32[]{:S(2)}) async-start(f32[32,24,128]{2,1,0:T(8,128)} %decode_attention.1), calls=%async_computation.2 | async-start | bytes 786432 | tf_op jit(solution)/shard_map/all_to_all | solution.py:335
  112.0 0.1 copy.11
  112.1 0.1 eq.27
  112.2 0.8 select_reduce_fusion.logical_ref
  113.1 0.0 all-gather.3.cloned.1.call-done
  113.1 10.0 %project.3 = bf16[256,640]{1,0:T(8,128)(2,1)S(1)} custom-call(s32[4]{0:T(128)S(1)} %copy-done.7, s32[32]{0:T(128)S(1)} %select_reduce_fusion.logical_ref, bf16[512,1024]{1,0:T(8,128)(2,1)S(1)} %pack.2.refs_0_, bf16[512,1024]{1,0:T(8,128)(2,1)S(1)} %collective-permute-done.11.refs_1_, bf16[512,1024]{1,0:T(8,128)(2,1)} %collective-permute-done.12.refs_2_, ...), custom_call_target="tpu_custom_call" | custom-call | flops 2684354560 | bytes 15000000 | tf_op jit(solution)/shard_map/project/pallas_call | solution.py:154
  123.1 0.7 copy-done.5
  123.8 2.3 %all-to-all-done.2.in_ref = f32[32,24,128]{2,1,0:T(8,128)S(1)} async-done(((f32[32,24,128]{2,1,0:T(8,128)}), f32[32,24,128]{2,1,0:T(8,128)S(1)}, u32[]{:S(2)}, u32[]{:S(2)}) %all-to-all-start.2) | async-done | bytes 393248 | tf_op jit(solution)/shard_map/all_to_all | solution.py:335
  126.1 0.3 collective-permute-start.17
  126.4 0.3 decode_combine.1
  126.7 0.6 copy-done.4
  127.3 6.3 %all-to-all-start.3 = ((bf16[32,16,128]{2,1,0:T(8,128)(2,1)}), bf16[32,16,128]{2,1,0:T(8,128)(2,1)}, u32[]{:S(2)}, u32[]{:S(2)}) async-start(bf16[32,16,128]{2,1,0:T(8,128)(2,1)} %copy-done.4), calls=%async_computation.3 | async-start | bytes 262144 | tf_op jit(solution)/shard_map/all_to_all | solution.py:335
  133.7 9.7 %project.2.mine_ref = bf16[256,640]{1,0:T(8,128)(2,1)S(1)} custom-call(s32[4]{0:T(128)S(1)} %copy-done.7, s32[32]{0:T(128)S(1)} %select_reduce_fusion.logical_ref, bf16[512,1024]{1,0:T(8,128)(2,1)S(1)} %pack.2.refs_0_, bf16[512,1024]{1,0:T(8,128)(2,1)S(1)} %collective-permute-done.11.refs_1_, bf16[512,1024]{1,0:T(8,128)(2,1)} %collective-permute-done.12.refs_2_, ...), custom_call_target="tpu_custom_call" | custom-call | flops 2684354560 | bytes 15000000 | tf_op jit(solution)/shard_map/project/pallas_call | solution.py:154
  143.4 2.7 %prefill_attention.1 = (bf16[256,1024]{1,0:T(8,128)(2,1)}, bf16[48,1024]{1,0:T(8,128)(2,1)}) custom-call(s32[4]{0:T(128)S(1)} %copy-done.7, bf16[256,640]{1,0:T(8,128)(2,1)S(1)} %project.2.mine_ref, bf16[256,640]{1,0:T(8,128)(2,1)} %collective-permute-done.17.other_ref, bf16[32,16,128]{2,1,0:T(8,128)(2,1)} %all-to-all-done.3.decode_ref), custom_call_target="tpu_custom_call" | custom-call | flops 140000000 | bytes 1200000 | tf_op jit(solution)/shard_map/prefill_attention/pallas_call | solution.py:200
  (41 shorter events, 0.2 us)
Async XLA Ops:
  7.2 8.9 %copy-start.9 = (s32[32]{0:T(128)S(1)}, s32[32]{0:T(128)}, u32[]{:S(2)}) copy-start(s32[32]{0:T(128)} %param.15) | copy-start | bytes 388
  7.2 12.1 %copy-start.8 = (bf16[48,1024]{1,0:T(8,128)(2,1)S(1)}, bf16[48,1024]{1,0:T(8,128)(2,1)}, u32[]{:S(2)}) copy-start(bf16[48,1024]{1,0:T(8,128)(2,1)} %param.9) | copy-start | bytes 294916
  7.2 105.9 %all-gather.3.cloned.1.call-start = ((), (), s32[]{:S(2)}) async-start(), calls=%async_computation.4 | async-start | bytes 11141120 | tf_op jit(solution)/shard_map/all_gather | solution.py:356
  7.2 31.5 %copy-start.1 = (bf16[256,1024]{1,0:T(8,128)(2,1)S(1)}, bf16[256,1024]{1,0:T(8,128)(2,1)}, u32[]{:S(2)}) copy-start(bf16[256,1024]{1,0:T(8,128)(2,1)} %qw_ref.3) | copy-start | bytes 1572868
  7.2 31.5 %copy-start.3 = (bf16[256,256]{1,0:T(8,128)(2,1)S(1)}, bf16[256,256]{1,0:T(8,128)(2,1)}, u32[]{:S(2)}) copy-start(bf16[256,256]{1,0:T(8,128)(2,1)} %kv_ref.3) | copy-start | bytes 393220
  8.4 17.1 %collective-permute-start.2 = (bf16[128,1024]{1,0:T(8,128)(2,1)S(1)}, bf16[128,1024]{1,0:T(8,128)(2,1)S(1)}, u32[]{:S(2)}, u32[]{:S(2)}) collective-permute-start(bf16[128,1024]{1,0:T(8,128)(2,1)S(1)} %get-tuple-element.32.refs_0_), channel_id=1, source_target_pairs={{0,1},{1,2},{2,3},{3,0},{4,5},{5,6},{6,7},{7,4},{8,9},{9,10},{10,1... | collective-permute-start | bytes 786440 | tf_op jit(solution)/shard_map/ppermute | solution.py:38
  10.6 14.9 %collective-permute-start.3 = (bf16[128,1024]{1,0:T(8,128)(2,1)S(1)}, bf16[128,1024]{1,0:T(8,128)(2,1)S(1)}, u32[]{:S(2)}, u32[]{:S(2)}) collective-permute-start(bf16[128,1024]{1,0:T(8,128)(2,1)S(1)} %get-tuple-element.32.refs_0_), channel_id=1, source_target_pairs={{0,3},{1,0},{2,1},{3,2},{4,7},{5,4},{6,5},{7,6},{8,11},{9,8},{10,9... | collective-permute-start | bytes 786440 | tf_op jit(solution)/shard_map/ppermute | solution.py:38
  12.2 1.0 copy-start
  13.2 0.9 copy-start.2
  14.1 25.5 %copy-start.6 = (s32[4]{0:T(128)}, s32[4]{0:T(128)S(1)}, u32[]{:S(2)}) copy-start(s32[4]{0:T(128)S(1)} %pad_add_fusion.1.place_ref) | copy-start | bytes 52
  14.8 10.7 %collective-permute-start = (bf16[256,640]{1,0:T(8,128)(2,1)S(1)}, bf16[256,640]{1,0:T(8,128)(2,1)S(1)}, u32[]{:S(2)}, u32[]{:S(2)}) collective-permute-start(bf16[256,640]{1,0:T(8,128)(2,1)S(1)} %get-tuple-element.24), channel_id=1, source_target_pairs={{0,128},{128,0},{1,129},{129,1},{2,130},{130,2},{3,131},{131,3},{4... | collective-permute-start | bytes 983048 | tf_op jit(solution)/shard_map/ppermute | solution.py:38
  19.3 6.2 %collective-permute-start.1 = (bf16[48,256]{1,0:T(8,128)(2,1)S(1)}, bf16[48,256]{1,0:T(8,128)(2,1)S(1)}, u32[]{:S(2)}, u32[]{:S(2)}) collective-permute-start(bf16[48,256]{1,0:T(8,128)(2,1)S(1)} %dynamic-slice_select_fusion), channel_id=1, source_target_pairs={{0,4},{4,0},{1,5},{5,1},{2,6},{6,2},{3,7},{7,3},{8,12},{12,8},{9,1... | collective-permute-start | bytes 73736 | tf_op jit(solution)/shard_map/ppermute | solution.py:38
  26.4 4.9 %collective-permute-start.6 = (bf16[48,256]{1,0:T(8,128)(2,1)S(1)}, bf16[48,256]{1,0:T(8,128)(2,1)S(1)}, u32[]{:S(2)}, u32[]{:S(2)}) collective-permute-start(bf16[48,256]{1,0:T(8,128)(2,1)S(1)} %fusion.2), channel_id=1, source_target_pairs={{0,2},{1,3},{2,0},{3,1},{4,6},{5,7},{6,4},{7,5},{8,10},{9,11},{10,... | collective-permute-start | bytes 73736 | tf_op jit(solution)/shard_map/ppermute | solution.py:38
  27.9 4.9 %collective-permute-start.5 = (bf16[48,256]{1,0:T(8,128)(2,1)S(1)}, bf16[48,256]{1,0:T(8,128)(2,1)S(1)}, u32[]{:S(2)}, u32[]{:S(2)}) collective-permute-start(bf16[48,256]{1,0:T(8,128)(2,1)S(1)} %fusion.2), channel_id=1, source_target_pairs={{0,3},{1,0},{2,1},{3,2},{4,7},{5,4},{6,5},{7,6},{8,11},{9,8},{10,9... | collective-permute-start | bytes 73736 | tf_op jit(solution)/shard_map/ppermute | solution.py:38
  28.7 11.0 %collective-permute-start.7 = (bf16[128,1024]{1,0:T(8,128)(2,1)S(1)}, bf16[128,1024]{1,0:T(8,128)(2,1)S(1)}, u32[]{:S(2)}, u32[]{:S(2)}) collective-permute-start(bf16[128,1024]{1,0:T(8,128)(2,1)S(1)} %get-tuple-element.28.refs_0_), channel_id=1, source_target_pairs={{0,128},{128,4},{4,132},{132,0},{1,129},{129,5},{5,133},{133,1},{2... | collective-permute-start | bytes 786440 | tf_op jit(solution)/shard_map/ppermute | solution.py:38
  28.7 11.0 %collective-permute-start.8 = (bf16[128,1024]{1,0:T(8,128)(2,1)S(1)}, bf16[128,1024]{1,0:T(8,128)(2,1)S(1)}, u32[]{:S(2)}, u32[]{:S(2)}) collective-permute-start(bf16[128,1024]{1,0:T(8,128)(2,1)S(1)} %get-tuple-element.28.refs_0_), channel_id=1, source_target_pairs={{0,132},{128,0},{4,128},{132,4},{1,133},{129,1},{5,129},{133,5},{2... | collective-permute-start | bytes 786440 | tf_op jit(solution)/shard_map/ppermute | solution.py:38
  31.4 9.8 %collective-permute-start.9 = (bf16[128,1024]{1,0:T(8,128)(2,1)S(1)}, bf16[128,1024]{1,0:T(8,128)(2,1)S(1)}, u32[]{:S(2)}, u32[]{:S(2)}) collective-permute-start(bf16[128,1024]{1,0:T(8,128)(2,1)S(1)} %get-tuple-element.28.refs_0_), channel_id=1, source_target_pairs={{0,4},{128,132},{4,0},{132,128},{1,5},{129,133},{5,1},{133,129},{2... | collective-permute-start | bytes 786440 | tf_op jit(solution)/shard_map/ppermute | solution.py:38
  31.4 9.8 %collective-permute-start.10 = (bf16[128,1024]{1,0:T(8,128)(2,1)S(1)}, bf16[128,1024]{1,0:T(8,128)(2,1)S(1)}, u32[]{:S(2)}, u32[]{:S(2)}) collective-permute-start(bf16[128,1024]{1,0:T(8,128)(2,1)S(1)} %get-tuple-element.32.refs_0_), channel_id=1, source_target_pairs={{0,2},{1,3},{2,0},{3,1},{4,6},{5,7},{6,4},{7,5},{8,10},{9,11},{10,... | collective-permute-start | bytes 786440 | tf_op jit(solution)/shard_map/ppermute | solution.py:38
  32.8 5.9 %collective-permute-start.4 = (bf16[48,256]{1,0:T(8,128)(2,1)S(1)}, bf16[48,256]{1,0:T(8,128)(2,1)S(1)}, u32[]{:S(2)}, u32[]{:S(2)}) collective-permute-start(bf16[48,256]{1,0:T(8,128)(2,1)S(1)} %fusion.2), channel_id=1, source_target_pairs={{0,1},{1,2},{2,3},{3,0},{4,5},{5,6},{6,7},{7,4},{8,9},{9,10},{10,1... | collective-permute-start | bytes 73736 | tf_op jit(solution)/shard_map/ppermute | solution.py:38
  41.3 30.0 %collective-permute-start.14 = (bf16[512,1024]{1,0:T(8,128)(2,1)S(1)}, bf16[512,1024]{1,0:T(8,128)(2,1)}, u32[]{:S(2)}, u32[]{:S(2)}) collective-permute-start(bf16[512,1024]{1,0:T(8,128)(2,1)S(1)} %pack.3.refs_4_), channel_id=1, source_target_pairs={{0,128},{128,4},{4,132},{132,0},{1,129},{129,5},{5,133},{133,1},{2... | collective-permute-start | bytes 3145736 | tf_op jit(solution)/shard_map/ppermute | solution.py:38
  41.4 29.9 %collective-permute-start.15 = (bf16[512,1024]{1,0:T(8,128)(2,1)S(1)}, bf16[512,1024]{1,0:T(8,128)(2,1)}, u32[]{:S(2)}, u32[]{:S(2)}) collective-permute-start(bf16[512,1024]{1,0:T(8,128)(2,1)S(1)} %pack.3.refs_4_), channel_id=1, source_target_pairs={{0,132},{128,0},{4,128},{132,4},{1,133},{129,1},{5,129},{133,5},{2... | collective-permute-start | bytes 3145736 | tf_op jit(solution)/shard_map/ppermute | solution.py:38
  44.0 27.2 %all-to-all-start = ((f32[64,8,128]{2,1,0:T(8,128)}), f32[64,8,128]{2,1,0:T(8,128)S(1)}, u32[]{:S(2)}, u32[]{:S(2)}) async-start(f32[64,8,128]{2,1,0:T(8,128)} %decode_partial.1), calls=%async_computation | async-start | bytes 524288 | tf_op jit(solution)/shard_map/all_to_all | solution.py:335
  56.8 56.3 %collective-permute-start.11 = (bf16[512,1024]{1,0:T(8,128)(2,1)S(1)}, bf16[512,1024]{1,0:T(8,128)(2,1)S(1)}, u32[]{:S(2)}, u32[]{:S(2)}) collective-permute-start(bf16[512,1024]{1,0:T(8,128)(2,1)S(1)} %pack.2.refs_0_), channel_id=1, source_target_pairs={{0,1},{1,2},{2,3},{3,0},{4,5},{5,6},{6,7},{7,4},{8,9},{9,10},{10,1... | collective-permute-start | bytes 3145736 | tf_op jit(solution)/shard_map/ppermute | solution.py:38
  57.5 55.5 %collective-permute-start.12 = (bf16[512,1024]{1,0:T(8,128)(2,1)S(1)}, bf16[512,1024]{1,0:T(8,128)(2,1)}, u32[]{:S(2)}, u32[]{:S(2)}) collective-permute-start(bf16[512,1024]{1,0:T(8,128)(2,1)S(1)} %pack.2.refs_0_), channel_id=1, source_target_pairs={{0,3},{1,0},{2,1},{3,2},{4,7},{5,4},{6,5},{7,6},{8,11},{9,8},{10,9... | collective-permute-start | bytes 3145736 | tf_op jit(solution)/shard_map/ppermute | solution.py:38
  59.5 53.5 %collective-permute-start.13 = (bf16[512,1024]{1,0:T(8,128)(2,1)S(1)}, bf16[512,1024]{1,0:T(8,128)(2,1)}, u32[]{:S(2)}, u32[]{:S(2)}) collective-permute-start(bf16[512,1024]{1,0:T(8,128)(2,1)S(1)} %pack.2.refs_0_), channel_id=1, source_target_pairs={{0,2},{1,3},{2,0},{3,1},{4,6},{5,7},{6,4},{7,5},{8,10},{9,11},{10,... | collective-permute-start | bytes 3145736 | tf_op jit(solution)/shard_map/ppermute | solution.py:38
  71.3 41.7 %collective-permute-start.16 = (bf16[512,1024]{1,0:T(8,128)(2,1)S(1)}, bf16[512,1024]{1,0:T(8,128)(2,1)}, u32[]{:S(2)}, u32[]{:S(2)}) collective-permute-start(bf16[512,1024]{1,0:T(8,128)(2,1)S(1)} %pack.3.refs_4_), channel_id=1, source_target_pairs={{0,4},{128,132},{4,0},{132,128},{1,5},{129,133},{5,1},{133,129},{2... | collective-permute-start | bytes 3145736 | tf_op jit(solution)/shard_map/ppermute | solution.py:38
  98.2 14.9 %copy-start.7 = (s32[4]{0:T(128)S(1)}, s32[4]{0:T(128)}, u32[]{:S(2)}) copy-start(s32[4]{0:T(128)} %copy-done.6) | copy-start | bytes 52
  102.9 23.2 %all-to-all-start.2 = ((f32[32,24,128]{2,1,0:T(8,128)}), f32[32,24,128]{2,1,0:T(8,128)S(1)}, u32[]{:S(2)}, u32[]{:S(2)}) async-start(f32[32,24,128]{2,1,0:T(8,128)} %decode_attention.1), calls=%async_computation.2 | async-start | bytes 786432 | tf_op jit(solution)/shard_map/all_to_all | solution.py:335
  123.1 0.7 copy-start.5
  126.1 17.4 %collective-permute-start.17 = (bf16[256,640]{1,0:T(8,128)(2,1)}, bf16[256,640]{1,0:T(8,128)(2,1)}, u32[]{:S(2)}, u32[]{:S(2)}) collective-permute-start(bf16[256,640]{1,0:T(8,128)(2,1)} %copy-done.5), channel_id=1, source_target_pairs={{0,128},{128,0},{1,129},{129,1},{2,130},{130,2},{3,131},{131,3},{4... | collective-permute-start | bytes 983048 | tf_op jit(solution)/shard_map/ppermute | solution.py:38
  126.7 0.7 copy-start.4
  127.3 16.1 %all-to-all-start.3 = ((bf16[32,16,128]{2,1,0:T(8,128)(2,1)}), bf16[32,16,128]{2,1,0:T(8,128)(2,1)}, u32[]{:S(2)}, u32[]{:S(2)}) async-start(bf16[32,16,128]{2,1,0:T(8,128)(2,1)} %copy-done.4), calls=%async_computation.3 | async-start | bytes 262144 | tf_op jit(solution)/shard_map/all_to_all | solution.py:335
Sparse Core Ops, SparseCore 0:
  26.6 76.0 all-gather.2
